TPU v7x, 128 devices: a whole 4x4x4 slice. The times are simulated.
128 devices in a mesh: dp: 16 (over y, z), et: 8 (over x, core).
Axes of the slice: x: 4, y: 4, z: 4, core: 2. Of those that a mesh axis runs over, the one named last changes fastest.
Arguments:
- tokens: bfloat16 [2048, 4096], P('dp', 'et'), may hold values from -6 to 6
- routes: int32 [2048, 2], P('dp'), may hold values from 0 to 7, all different within a row; in each aligned block of 128 rows (0 to 127, 128 to 255, ...) at most 40 rows name the same one
- route_probs: float32 [2048, 2], P('dp'), may hold values from 0.2 to 1
- grad_out: bfloat16 [2048, 4096], P('dp', 'et'), may hold values from -6 to 6
- w_gate: bfloat16 [57344, 4096], P(('dp', 'et')), may hold values from -0.09375 to 0.09375
- w_up: bfloat16 [57344, 4096], P(('dp', 'et')), may hold values from -0.09375 to 0.09375
- w_down: bfloat16 [57344, 4096], P(('dp', 'et')), may hold values from -0.046875 to 0.046875
Outputs:
- layer_out: bfloat16 [2048, 4096], P('dp', 'et')
- grad_tokens: bfloat16 [2048, 4096], P('dp', 'et')
- grad_gate: bfloat16 [57344, 4096], P(('dp', 'et'))
- grad_up: bfloat16 [57344, 4096], P(('dp', 'et'))
- grad_down: bfloat16 [57344, 4096], P(('dp', 'et'))
Inputs may be any that keep to these rules, and one draw needn't show every extreme that they name: `routes`: each row names 2 different experts of 8; within each aligned block of 128 rows (the tokens of one index of dp) no expert is named by more than 40 rows.
All inputs are finite; a program needn't handle non-finite values.
Results may differ from a plain program's by a relative error of at most 0.0058.
Values may be sent and summed in bfloat16 or wider, within the bound.
A program may use at most 192 MiB of HBM per device.

v0:
```python
import jax
import jax.numpy as jnp
from jax import lax
from jax.sharding import PartitionSpec as P

EXP = 4
TILE = 128
CAP = 40


def route_tables(routes, route_probs):
    labels = jnp.arange(EXP, dtype=jnp.int32)
    matches = routes[:, :, None] == labels[None, None, :]
    member = jnp.sum(matches.astype(jnp.int32), axis=1)
    weight = jnp.sum(jnp.where(matches, route_probs[:, :, None], 0.0), axis=1)
    placed = jnp.cumsum(member, axis=0) - member
    slot_ids = jnp.arange(CAP, dtype=jnp.int32)
    pick_table = (member[None, :, :] == 1) & (placed[None, :, :] == slot_ids[:, None, None])
    pick_table = jnp.transpose(pick_table, (2, 0, 1)).astype(jnp.float32)
    expert_loads = jnp.sum(member, axis=0)
    return (pick_table, weight, expert_loads)


def pack_rows(pick_table, weight, features_in, cotangent, group_size):
    picks_low = pick_table.astype(jnp.bfloat16)
    chosen = jnp.einsum(
        "ect,td->ecd", picks_low, features_in, preferred_element_type=jnp.float32
    ).astype(jnp.bfloat16)
    chosen_cot = jnp.einsum("ect,td->ecd", picks_low, cotangent, preferred_element_type=jnp.float32)
    chosen_weight = jnp.einsum("ect,te->ec", pick_table, weight, precision=lax.Precision.HIGHEST)
    scaled = (chosen_weight[:, :, None] * chosen_cot).astype(jnp.bfloat16)
    return (jnp.repeat(chosen, group_size, axis=0), jnp.repeat(scaled, group_size, axis=0))


def expert_work(recv_x, recv_dy, counts, w_gate, w_up, w_down):
    sources, capacity, feature_count = recv_x.shape
    total_rows = sources * capacity
    flat_x = recv_x.reshape(total_rows, feature_count)
    flat_dy = recv_dy.reshape(total_rows, feature_count)
    slot_ends = jnp.cumsum(counts)
    slot_starts = slot_ends - counts
    live_rows = slot_ends[-1]
    tiles_max = -(-total_rows // TILE)
    padded = tiles_max * TILE
    positions = jnp.arange(padded, dtype=jnp.int32)
    source_ids = jnp.arange(sources, dtype=jnp.int32)
    source_of = jnp.sum((slot_ends[None, :] <= positions[:, None]).astype(jnp.int32), axis=1)
    source_of = jnp.minimum(source_of, sources - 1)
    start_of = jnp.sum(
        jnp.where(source_ids[None, :] == source_of[:, None], slot_starts[None, :], 0), axis=1
    )
    row_of = source_of * capacity + positions - start_of
    row_of = jnp.where(positions < live_rows, row_of, total_rows)
    hidden_units = w_gate.shape[0]
    contract_last = (((1,), (1,)), ((), ()))
    contract_first = (((0,), (0,)), ((), ()))

    def one_tile(tile_step, running):
        out_rows, dx_rows, acc_gate, acc_up, acc_down = running
        row_index = lax.dynamic_slice_in_dim(row_of, tile_step * TILE, TILE)
        tile_x = jnp.take(flat_x, row_index, axis=0, mode="fill", fill_value=0)
        tile_dy = jnp.take(flat_dy, row_index, axis=0, mode="fill", fill_value=0)
        gate_pre = lax.dot_general(
            tile_x, w_gate, contract_last, preferred_element_type=jnp.float32
        )
        up_pre = lax.dot_general(tile_x, w_up, contract_last, preferred_element_type=jnp.float32)
        squash = jax.nn.sigmoid(gate_pre)
        active = gate_pre * squash
        hidden = (active * up_pre).astype(jnp.bfloat16)
        out_tile = jnp.dot(hidden, w_down, preferred_element_type=jnp.float32)
        d_hidden = lax.dot_general(
            tile_dy, w_down, contract_last, preferred_element_type=jnp.float32
        )
        d_gate = (d_hidden * up_pre * squash * (1.0 + gate_pre * (1.0 - squash))).astype(
            jnp.bfloat16
        )
        d_up = (d_hidden * active).astype(jnp.bfloat16)
        dx_tile = jnp.dot(d_gate, w_gate, preferred_element_type=jnp.float32) + jnp.dot(
            d_up, w_up, preferred_element_type=jnp.float32
        )
        acc_gate = acc_gate + lax.dot_general(
            d_gate, tile_x, contract_first, preferred_element_type=jnp.float32
        )
        acc_up = acc_up + lax.dot_general(
            d_up, tile_x, contract_first, preferred_element_type=jnp.float32
        )
        acc_down = acc_down + lax.dot_general(
            hidden, tile_dy, contract_first, preferred_element_type=jnp.float32
        )
        out_rows = out_rows.at[row_index].set(out_tile, mode="drop")
        dx_rows = dx_rows.at[row_index].set(dx_tile, mode="drop")
        return (out_rows, dx_rows, acc_gate, acc_up, acc_down)

    empty_rows = jnp.zeros((total_rows, feature_count), jnp.float32)
    empty_grad = jnp.zeros((hidden_units, feature_count), jnp.float32)
    tile_count = (live_rows + TILE - 1) // TILE
    out_rows, dx_rows, acc_gate, acc_up, acc_down = lax.fori_loop(
        0, tile_count, one_tile, (empty_rows, empty_rows, empty_grad, empty_grad, empty_grad)
    )
    shaped = (sources, capacity, feature_count)
    return (
        out_rows.reshape(shaped),
        dx_rows.reshape(shaped),
        acc_gate.astype(jnp.bfloat16),
        acc_up.astype(jnp.bfloat16),
        acc_down.astype(jnp.bfloat16),
    )


def spread_back(pick_table, weight, back_out, back_dx, group_size):
    grouped = (EXP, group_size, back_out.shape[1], back_out.shape[2])
    per_out = jnp.sum(back_out.reshape(grouped), axis=1)
    per_dx = jnp.sum(back_dx.reshape(grouped), axis=1)
    layer_part = jnp.einsum(
        "ect,te,ecd->td", pick_table, weight, per_out, precision=lax.Precision.HIGHEST
    )
    dx_part = jnp.einsum("ect,ecd->td", pick_table, per_dx, precision=lax.Precision.HIGHEST)
    return (layer_part, dx_part)


def per_device(tokens, routes, route_probs, grad_out, w_gate, w_up, w_down):
    group_size = lax.axis_size("dp") // EXP
    my_expert = lax.axis_index("dp") // group_size
    pick_table, weight, expert_loads = route_tables(routes, route_probs)
    load_rows = lax.all_gather(expert_loads[None, :], "dp", axis=0, tiled=True)
    labels = jnp.arange(EXP, dtype=jnp.int32)
    counts = jnp.sum(jnp.where(labels[None, :] == my_expert, load_rows, 0), axis=1)
    full_x, full_dy = (
        lax.all_gather(tokens, "et", axis=1, tiled=True),
        lax.all_gather(grad_out, "et", axis=1, tiled=True),
    )
    send_x, send_dy = pack_rows(pick_table, weight, full_x, full_dy, group_size)
    recv_x, recv_dy = (
        lax.all_to_all(send_x, "dp", split_axis=0, concat_axis=0, tiled=True),
        lax.all_to_all(send_dy, "dp", split_axis=0, concat_axis=0, tiled=True),
    )
    out_rows, dx_rows, grad_gate, grad_up, grad_down = expert_work(
        recv_x, recv_dy, counts, w_gate, w_up, w_down
    )
    back_out, back_dx = (
        lax.all_to_all(out_rows, "dp", split_axis=0, concat_axis=0, tiled=True),
        lax.all_to_all(dx_rows, "dp", split_axis=0, concat_axis=0, tiled=True),
    )
    layer_part, dx_part = spread_back(pick_table, weight, back_out, back_dx, group_size)
    layer_sum, dx_sum = (
        lax.psum_scatter(layer_part, "et", scatter_dimension=1, tiled=True),
        lax.psum_scatter(dx_part, "et", scatter_dimension=1, tiled=True),
    )
    return (
        layer_sum.astype(jnp.bfloat16),
        dx_sum.astype(jnp.bfloat16),
        grad_gate,
        grad_up,
        grad_down,
    )


def solution(mesh):
    placed = (
        P("dp", "et"),
        P("dp", None),
        P("dp", None),
        P("dp", "et"),
        P(("dp", "et"), None),
        P(("dp", "et"), None),
        P(("dp", "et"), None),
    )
    return jax.shard_map(
        per_device,
        mesh=mesh,
        in_specs=placed,
        out_specs=(
            P("dp", "et"),
            P("dp", "et"),
            P(("dp", "et"), None),
            P(("dp", "et"), None),
            P(("dp", "et"), None),
        ),
        check_vma=False,
    )
```

profile of v0, /device:TPU:0, one launch (start us, length us, event | category | flops | bytes accessed | tf_op | source)
XLA Modules:
  0.0 920.6 jit_solution(494574225322511276)
XLA Ops:
  9.1 26.4 %all-gather.4.cloned.1.call-done = bf16[128,4096]{1,0:T(8,128)(2,1)} async-done(((bf16[128,512]{1,0:T(8,128)(2,1)}), bf16[128,4096]{1,0:T(8,128)(2,1)}) %all-gather.4.cloned.1.call-update) | async-done | bytes 1048592 | tf_op jit(solution)/shard_map/all_gather | solution.py:129
  48.9 24.4 %all-gather.6.cloned.1.call-done = bf16[128,4096]{1,0:T(8,128)(2,1)} async-done(((bf16[128,512]{1,0:T(8,128)(2,1)}), bf16[128,4096]{1,0:T(8,128)(2,1)}) %all-gather.6.cloned.1.call-update) | async-done | bytes 1048592 | tf_op jit(solution)/shard_map/all_gather | solution.py:130
  75.1 49.4 %all-to-all-done = bf16[16,40,4096]{2,1,0:T(8,128)(2,1)} async-done(((bf16[16,40,4096]{2,1,0:T(8,128)(2,1)}), bf16[16,40,4096]{2,1,0:T(8,128)(2,1)}, u32[]{:S(2)}, u32[]{:S(2)}) %all-to-all-start) | async-done | bytes 5242912 | tf_op jit(solution)/shard_map/all_to_all | solution.py:134
  127.5 14.5 %all-to-all-start.1 = ((bf16[16,40,4096]{2,1,0:T(8,128)(2,1)}), bf16[16,40,4096]{2,1,0:T(8,128)(2,1)}, u32[]{:S(2)}, u32[]{:S(2)}) async-start(bf16[16,40,4096]{2,1,0:T(8,128)(2,1)} %bitcast.82), calls=%async_computation.1 | async-start | bytes 10485760 | tf_op jit(solution)/shard_map/all_to_all | solution.py:135
  143.5 81.2 %all-reduce = s32[64]{0:T(128)S(1)} all-reduce(s32[64]{0:T(128)S(1)} %dynamic-update-slice), channel_id=2, replica_groups=mesh['dp'=16,'et'=8] {'dp'}, use_global_device_ids=true, to_apply=%add | all-reduce | flops 64 | bytes 512
  249.2 320.5 %while.18 = (s32[]{:T(128)}, f32[640,4096]{1,0:T(8,128)}, f32[640,4096]{1,0:T(8,128)}, f32[448,4096]{1,0:T(8,128)}, f32[448,4096]{1,0:T(8,128)}, /*index=5*/f32[...) while((s32[]{:T(128)}, f32[640,4096]{1,0:T(8,128)}, ...), condition=%wide.region_11.13_spmd, body=%wide.region_8.12_spmd.sunk | while | flops 4237895424 | bytes 217965392 | solution.py:97
  275.9 9.8 %convolution_add_fusion.10 = f32[448,4096]{1,0:T(8,128)} fusion(f32[448,4096]{1,0:T(8,128)} %get-tuple-element.227, bf16[128,448]{0,1:T(8,128)(2,1)S(1)} %get-tuple-element.205, bf16[128,4096]{1,0:T(8,128)(2,1)S(1)} %gather_fusion, pred[128]{0:T(512)(128)(4,1)S(1)} %get-tuple-element.202), kind=kOutput, calls=%fused_computation.5.clone.1 | convolution fusion | flops 472121344 | bytes 15843456 | tf_op jit(solution)/shard_map/while/body/dot_general | solution.py:84
  293.1 10.6 %scatter_fusion.1 = f32[640,4096]{1,0:T(8,128)} fusion(f32[640,4096]{1,0:T(8,128)} %get-tuple-element.225, s32[128]{0:T(128)S(1)} %get-tuple-element.201, f32[128,4096]{1,0:T(8,128)} %convolution_add_fusion.8), kind=kCustom, calls=%fused_computation.3.clone.1 | custom fusion | bytes 6291968 | tf_op jit(solution)/shard_map/while/body/scatter | solution.py:91
  303.6 9.7 %scatter_fusion = f32[640,4096]{1,0:T(8,128)} fusion(f32[640,4096]{1,0:T(8,128)} %get-tuple-element.224, s32[128]{0:T(128)S(1)} %get-tuple-element.201, f32[128,4096]{1,0:T(8,128)S(1)} %fusion.76), kind=kCustom, calls=%fused_computation.2.clone.1 | custom fusion | bytes 6291968 | tf_op jit(solution)/shard_map/while/body/scatter | solution.py:90
  340.0 9.8 %convolution_add_fusion.10 = f32[448,4096]{1,0:T(8,128)} fusion(f32[448,4096]{1,0:T(8,128)} %get-tuple-element.227, bf16[128,448]{0,1:T(8,128)(2,1)S(1)} %get-tuple-element.205, bf16[128,4096]{1,0:T(8,128)(2,1)S(1)} %gather_fusion, pred[128]{0:T(512)(128)(4,1)S(1)} %get-tuple-element.202), kind=kOutput, calls=%fused_computation.5.clone.1 | convolution fusion | flops 472121344 | bytes 15843456 | tf_op jit(solution)/shard_map/while/body/dot_general | solution.py:84
  357.2 10.6 %scatter_fusion.1 = f32[640,4096]{1,0:T(8,128)} fusion(f32[640,4096]{1,0:T(8,128)} %get-tuple-element.225, s32[128]{0:T(128)S(1)} %get-tuple-element.201, f32[128,4096]{1,0:T(8,128)} %convolution_add_fusion.8), kind=kCustom, calls=%fused_computation.3.clone.1 | custom fusion | bytes 6291968 | tf_op jit(solution)/shard_map/while/body/scatter | solution.py:91
  367.7 9.7 %scatter_fusion = f32[640,4096]{1,0:T(8,128)} fusion(f32[640,4096]{1,0:T(8,128)} %get-tuple-element.224, s32[128]{0:T(128)S(1)} %get-tuple-element.201, f32[128,4096]{1,0:T(8,128)S(1)} %fusion.76), kind=kCustom, calls=%fused_computation.2.clone.1 | custom fusion | bytes 6291968 | tf_op jit(solution)/shard_map/while/body/scatter | solution.py:90
  404.1 9.8 %convolution_add_fusion.10 = f32[448,4096]{1,0:T(8,128)} fusion(f32[448,4096]{1,0:T(8,128)} %get-tuple-element.227, bf16[128,448]{0,1:T(8,128)(2,1)S(1)} %get-tuple-element.205, bf16[128,4096]{1,0:T(8,128)(2,1)S(1)} %gather_fusion, pred[128]{0:T(512)(128)(4,1)S(1)} %get-tuple-element.202), kind=kOutput, calls=%fused_computation.5.clone.1 | convolution fusion | flops 472121344 | bytes 15843456 | tf_op jit(solution)/shard_map/while/body/dot_general | solution.py:84
  421.3 10.6 %scatter_fusion.1 = f32[640,4096]{1,0:T(8,128)} fusion(f32[640,4096]{1,0:T(8,128)} %get-tuple-element.225, s32[128]{0:T(128)S(1)} %get-tuple-element.201, f32[128,4096]{1,0:T(8,128)} %convolution_add_fusion.8), kind=kCustom, calls=%fused_computation.3.clone.1 | custom fusion | bytes 6291968 | tf_op jit(solution)/shard_map/while/body/scatter | solution.py:91
  431.8 9.7 %scatter_fusion = f32[640,4096]{1,0:T(8,128)} fusion(f32[640,4096]{1,0:T(8,128)} %get-tuple-element.224, s32[128]{0:T(128)S(1)} %get-tuple-element.201, f32[128,4096]{1,0:T(8,128)S(1)} %fusion.76), kind=kCustom, calls=%fused_computation.2.clone.1 | custom fusion | bytes 6291968 | tf_op jit(solution)/shard_map/while/body/scatter | solution.py:90
  468.2 9.8 %convolution_add_fusion.10 = f32[448,4096]{1,0:T(8,128)} fusion(f32[448,4096]{1,0:T(8,128)} %get-tuple-element.227, bf16[128,448]{0,1:T(8,128)(2,1)S(1)} %get-tuple-element.205, bf16[128,4096]{1,0:T(8,128)(2,1)S(1)} %gather_fusion, pred[128]{0:T(512)(128)(4,1)S(1)} %get-tuple-element.202), kind=kOutput, calls=%fused_computation.5.clone.1 | convolution fusion | flops 472121344 | bytes 15843456 | tf_op jit(solution)/shard_map/while/body/dot_general | solution.py:84
  485.4 10.6 %scatter_fusion.1 = f32[640,4096]{1,0:T(8,128)} fusion(f32[640,4096]{1,0:T(8,128)} %get-tuple-element.225, s32[128]{0:T(128)S(1)} %get-tuple-element.201, f32[128,4096]{1,0:T(8,128)} %convolution_add_fusion.8), kind=kCustom, calls=%fused_computation.3.clone.1 | custom fusion | bytes 6291968 | tf_op jit(solution)/shard_map/while/body/scatter | solution.py:91
  495.9 9.7 %scatter_fusion = f32[640,4096]{1,0:T(8,128)} fusion(f32[640,4096]{1,0:T(8,128)} %get-tuple-element.224, s32[128]{0:T(128)S(1)} %get-tuple-element.201, f32[128,4096]{1,0:T(8,128)S(1)} %fusion.76), kind=kCustom, calls=%fused_computation.2.clone.1 | custom fusion | bytes 6291968 | tf_op jit(solution)/shard_map/while/body/scatter | solution.py:90
  532.3 9.8 %convolution_add_fusion.10 = f32[448,4096]{1,0:T(8,128)} fusion(f32[448,4096]{1,0:T(8,128)} %get-tuple-element.227, bf16[128,448]{0,1:T(8,128)(2,1)S(1)} %get-tuple-element.205, bf16[128,4096]{1,0:T(8,128)(2,1)S(1)} %gather_fusion, pred[128]{0:T(512)(128)(4,1)S(1)} %get-tuple-element.202), kind=kOutput, calls=%fused_computation.5.clone.1 | convolution fusion | flops 472121344 | bytes 15843456 | tf_op jit(solution)/shard_map/while/body/dot_general | solution.py:84
  549.4 10.6 %scatter_fusion.1 = f32[640,4096]{1,0:T(8,128)} fusion(f32[640,4096]{1,0:T(8,128)} %get-tuple-element.225, s32[128]{0:T(128)S(1)} %get-tuple-element.201, f32[128,4096]{1,0:T(8,128)} %convolution_add_fusion.8), kind=kCustom, calls=%fused_computation.3.clone.1 | custom fusion | bytes 6291968 | tf_op jit(solution)/shard_map/while/body/scatter | solution.py:91
  560.0 9.7 %scatter_fusion = f32[640,4096]{1,0:T(8,128)} fusion(f32[640,4096]{1,0:T(8,128)} %get-tuple-element.224, s32[128]{0:T(128)S(1)} %get-tuple-element.201, f32[128,4096]{1,0:T(8,128)S(1)} %fusion.76), kind=kCustom, calls=%fused_computation.2.clone.1 | custom fusion | bytes 6291968 | tf_op jit(solution)/shard_map/while/body/scatter | solution.py:90
  569.7 119.3 %all_to_all.20 = f32[16,40,4096]{2,1,0:T(8,128)} all-to-all(f32[16,40,4096]{2,1,0:T(8,128)} %bitcast.79), channel_id=1, replica_groups=mesh['dp'=16,'et'=8] {'dp'}, dimensions={0} | all-to-all | bytes 20971520 | tf_op jit(solution)/shard_map/all_to_all | solution.py:141
  704.9 165.2 %all-to-all-done.3 = f32[16,40,4096]{2,1,0:T(8,128)} async-done(((f32[16,40,4096]{2,1,0:T(8,128)}), f32[16,40,4096]{2,1,0:T(8,128)}, u32[]{:S(2)}, u32[]{:S(2)}) %all-to-all-start.3) | async-done | bytes 10485792 | tf_op jit(solution)/shard_map/all_to_all | solution.py:142
  896.1 16.4 %reduce-scatter.5.cloned.1.call-done = f32[128,512]{1,0:T(8,128)} async-done(((f32[128,4096]{1,0:T(8,128)}), f32[128,512]{1,0:T(8,128)}) %reduce-scatter.5.cloned.1.call-update) | async-done | bytes 262160 | tf_op jit(solution)/shard_map/reduce_scatter | solution.py:147
  (226 shorter events, 257.5 us)
Async XLA Ops:
  7.2 28.4 %all-gather.4.cloned.1.call-start = ((), (), s32[]{:S(2)}) async-start(), calls=%async_computation.6 | async-start | bytes 1179648 | tf_op jit(solution)/shard_map/all_gather | solution.py:129
  9.1 64.3 %copy-start.7 = (s32[4,128]{1,0:T(4,128)}, s32[4,128]{1,0:T(4,128)S(1)}, u32[]{:S(2)}) copy-start(s32[4,128]{1,0:T(4,128)S(1)} %copy.24) | copy-start | bytes 6148
  9.1 64.3 %copy-start.9 = (pred[4,128]{1,0:T(4,128)(4,1)}, pred[4,128]{1,0:T(4,128)(4,1)S(1)}, u32[]{:S(2)}) copy-start(pred[4,128]{1,0:T(4,128)(4,1)S(1)} %compare_bitcast_fusion) | copy-start | bytes 1540
  40.2 7.9 copy-start.13
  40.2 7.9 copy-start.14
  40.2 84.3 %all-to-all-start = ((bf16[16,40,4096]{2,1,0:T(8,128)(2,1)}), bf16[16,40,4096]{2,1,0:T(8,128)(2,1)}, u32[]{:S(2)}, u32[]{:S(2)}) async-start(bf16[16,40,4096]{2,1,0:T(8,128)(2,1)} %bitcast.83), calls=%async_computation | async-start | bytes 10485760 | tf_op jit(solution)/shard_map/all_to_all | solution.py:134
  47.4 26.0 %all-gather.6.cloned.1.call-start = ((), (), s32[]{:S(2)}) async-start(), calls=%async_computation.7 | async-start | bytes 1179648 | tf_op jit(solution)/shard_map/all_gather | solution.py:130
  127.5 14.5 %copy-start.15 = (u32[128]{0:T(128)S(1)}, u32[128]{0:T(128)}, u32[]{:S(2)}) copy-start(u32[128]{0:T(128)} %constant.82) | copy-start | bytes 1540
  127.5 99.7 %all-to-all-start.1 = ((bf16[16,40,4096]{2,1,0:T(8,128)(2,1)}), bf16[16,40,4096]{2,1,0:T(8,128)(2,1)}, u32[]{:S(2)}, u32[]{:S(2)}) async-start(bf16[16,40,4096]{2,1,0:T(8,128)(2,1)} %bitcast.82), calls=%async_computation.1 | async-start | bytes 10485760 | tf_op jit(solution)/shard_map/all_to_all | solution.py:135
  275.9 9.8 %copy-start = (f32[448,4096]{1,0:T(8,128)}, f32[448,4096]{1,0:T(8,128)S(1)}, u32[]{:S(2)}) copy-start(f32[448,4096]{1,0:T(8,128)S(1)} %convolution_add_fusion.11) | copy-start | bytes 22020100 | tf_op jit(solution)/shard_map/while
  328.7 3.7 copy-start.2
  340.0 9.8 %copy-start = (f32[448,4096]{1,0:T(8,128)}, f32[448,4096]{1,0:T(8,128)S(1)}, u32[]{:S(2)}) copy-start(f32[448,4096]{1,0:T(8,128)S(1)} %convolution_add_fusion.11) | copy-start | bytes 22020100 | tf_op jit(solution)/shard_map/while
  392.8 3.7 copy-start.2
  404.1 9.8 %copy-start = (f32[448,4096]{1,0:T(8,128)}, f32[448,4096]{1,0:T(8,128)S(1)}, u32[]{:S(2)}) copy-start(f32[448,4096]{1,0:T(8,128)S(1)} %convolution_add_fusion.11) | copy-start | bytes 22020100 | tf_op jit(solution)/shard_map/while
  456.9 3.7 copy-start.2
  468.2 9.8 %copy-start = (f32[448,4096]{1,0:T(8,128)}, f32[448,4096]{1,0:T(8,128)S(1)}, u32[]{:S(2)}) copy-start(f32[448,4096]{1,0:T(8,128)S(1)} %convolution_add_fusion.11) | copy-start | bytes 22020100 | tf_op jit(solution)/shard_map/while
  521.0 3.7 copy-start.2
  532.3 9.8 %copy-start = (f32[448,4096]{1,0:T(8,128)}, f32[448,4096]{1,0:T(8,128)S(1)}, u32[]{:S(2)}) copy-start(f32[448,4096]{1,0:T(8,128)S(1)} %convolution_add_fusion.11) | copy-start | bytes 22020100 | tf_op jit(solution)/shard_map/while
  689.0 181.1 %all-to-all-start.3 = ((f32[16,40,4096]{2,1,0:T(8,128)}), f32[16,40,4096]{2,1,0:T(8,128)}, u32[]{:S(2)}, u32[]{:S(2)}) async-start(f32[16,40,4096]{2,1,0:T(8,128)} %bitcast.78), calls=%async_computation.4 | async-start | bytes 20971520 | tf_op jit(solution)/shard_map/all_to_all | solution.py:142
  696.0 5.3 copy-start.8
  696.0 5.3 copy-start.10
  696.1 5.3 copy-start.12
  696.1 198.4 %reduce-scatter.3.cloned.1.call-start = ((), (), s32[]{:S(2)}) async-start(), calls=%async_computation.8 | async-start | bytes 2359296 | tf_op jit(solution)/shard_map/reduce_scatter | solution.py:146
  704.8 207.7 %reduce-scatter.5.cloned.1.call-start = ((), (), s32[]{:S(2)}) async-start(), calls=%async_computation.9 | async-start | bytes 2359296 | tf_op jit(solution)/shard_map/reduce_scatter | solution.py:147
  (37 other events, 112.8 us)
Sparse Core Ops, SparseCore 0:
  9.7 25.7 all-gather.3
  49.9 23.3 all-gather.5
  704.9 33.4 reduce-scatter.2
  878.2 34.2 reduce-scatter.4
where the time goes:
time: 923 us; the launch traced here: 921 us
  waiting for transfers between devices  283 us (31%)
  blocking collectives  201 us (22%)
  local copies, waits for them, and re-layouts  199 us (22%)
  matrix products  160 us (17%)
  other arithmetic  32.6 us (4%)
  starting transfers between devices  28.8 us (3%)
  between operations  15.3 us (2%)
    all_to_all x1, waiting for transfers between devices, per_device(): lax.all_to_all(dx_rows, 'dp', split_axis=0, concat_axis=0, tiled=True)  165 us
    all_to_all x1, blocking collectives, per_device(): lax.all_to_all(out_rows, 'dp', split_axis=0, concat_axis=0, tiled=True)  119 us
    unnamed x1, blocking collectives  81.2 us
    scatter x5, local copies, waits for them, and re-layouts, one_tile(): dx_rows = dx_rows.at[row_index].set(dx_tile, mode='drop')  52.8 us
    all_to_all x1, waiting for transfers between devices, per_device(): lax.all_to_all(send_x, 'dp', split_axis=0, concat_axis=0, tiled=True)  49.4 us
    dot_general x5, matrix products, one_tile(): lax.dot_general(d_up, tile_x, contract_first, preferred_element_type=jnp....  49.1 us
    scatter x5, local copies, waits for them, and re-layouts, one_tile(): out_rows = out_rows.at[row_index].set(out_tile, mode='drop')  48.3 us
    dot_general x5, matrix products, one_tile(): lax.dot_general(d_gate, tile_x, contract_first, preferred_element_type=jn...  36.6 us
  transfers between devices with their start and end apart: 7, of which 5 were waited for; matrix products, arithmetic and copies ran while one was open for 4% of the time, Pallas kernels for 0%

commit v1 on v0

v1 whole, which is shorter than its diff:
```python
import functools

import jax
import jax.numpy as jnp
from jax import lax
from jax.experimental import pallas as pl
from jax.experimental.pallas import tpu as pltpu
from jax.sharding import PartitionSpec as P

MESH = pl.DeviceIdType.MESH
EXP = 4
CAP = 40
SIDE = 4
ROWS = SIDE * CAP
HALF = ROWS // 2
KCH = 8
F32 = jnp.float32
BF16 = jnp.bfloat16
NT = (((1,), (1,)), ((), ()))
VMEM_LIMIT = 58 * 1024 * 1024


def place():
    dp = lax.axis_index("dp")
    et = lax.axis_index("et")
    return lax.div(dp, SIDE), lax.rem(dp, SIDE), lax.div(et, 2), lax.rem(et, 2)


def turn(value, by):
    return lax.rem(value + by, SIDE)


def device(y, z, x, c):
    return (y * SIDE + z, x * 2 + c)


def remote(src, dst, send_sem, recv_sem, target):
    return pltpu.make_async_remote_copy(
        src_ref=src, dst_ref=dst, send_sem=send_sem, recv_sem=recv_sem, device_id=target, device_id_type=MESH
    )


def greet(y, z, x, c):
    barrier = pltpu.get_barrier_semaphore()
    others = [device(y, z, x, 1 - c)]
    others += [device(y, z, turn(x, 1), c), device(y, z, turn(x, 3), c)]
    others += [device(y, turn(z, 1), x, c), device(y, turn(z, 3), x, c)]
    others += [device(turn(y, by), z, x, c) for by in (1, 2, 3)]
    for other in others:
        pl.semaphore_signal(barrier, inc=1, device_id=other, device_id_type=MESH)
    pl.semaphore_wait(barrier, len(others))


def pack_rows(routes, probs, tok, cot, pack):
    count = tok.shape[0]
    route = routes[...].astype(F32)
    prob = probs[...]
    square = (count, count)
    r0 = jnp.transpose(jnp.broadcast_to(route[:, 0:1], square))[:CAP]
    r1 = jnp.transpose(jnp.broadcast_to(route[:, 1:2], square))[:CAP]
    p0 = jnp.transpose(jnp.broadcast_to(prob[:, 0:1], square))[:CAP]
    p1 = jnp.transpose(jnp.broadcast_to(prob[:, 1:2], square))[:CAP]
    first = lax.broadcasted_iota(jnp.int32, square, 0)
    second = lax.broadcasted_iota(jnp.int32, square, 1)
    before = jnp.where(first < second, 1.0, 0.0).astype(BF16)
    slot = lax.broadcasted_iota(jnp.int32, (CAP, count), 0).astype(F32)
    x_all = tok[...]
    d_all = cot[...]
    for e in range(EXP):
        in0 = jnp.where(r0 == e, 1.0, 0.0)
        in1 = jnp.where(r1 == e, 1.0, 0.0)
        member = in0 + in1
        placed = jnp.dot(member.astype(BF16), before, preferred_element_type=F32)
        pick = jnp.where(placed == slot, member, 0.0)
        weight = jnp.sum(pick * (in0 * p0 + in1 * p1), axis=1, keepdims=True)
        pick = pick.astype(BF16)
        chosen = jnp.dot(pick, x_all, preferred_element_type=F32)
        scaled = weight * jnp.dot(pick, d_all, preferred_element_type=F32)
        pack[e] = jnp.concatenate([chosen, scaled], axis=0).astype(BF16)


def gather_kernel(
    routes, probs, tok, cot, wg, wu, wd, xg, sg, h_out, dg_out, du_out,
    pack, recv, xb, sb, wgv, wuv, wdv, acc_g, acc_u, acc_d,
    w_sem, out_sem, ys, yr, n1s, n1r, h1s, h1r, n2s, n2r, h2s, h2r, ps, pr,
):
    y, z, x, c = place()
    loads = []
    for i, (src, dst) in enumerate(((wg, wgv), (wu, wuv), (wd, wdv))):
        for k in range(KCH):
            load = pltpu.make_async_copy(src.at[:, pl.ds(k * 512, 512)], dst.at[k], w_sem.at[i, k])
            load.start()
            loads.append(load)
    pack_rows(routes, probs, tok, cot, pack)
    greet(y, z, x, c)
    sends = []
    y_copies = []
    for by in (1, 2, 3):
        e = turn(y, by)
        copy = remote(pack.at[e], recv.at[y], ys.at[by - 1], yr.at[by - 1], device(e, z, x, c))
        copy.start()
        sends.append(copy)
    recv[y] = pack[y]
    for by in (1, 2, 3):
        source = turn(y, SIDE - by)
        remote(pack.at[source], recv.at[source], ys.at[by - 1], yr.at[by - 1], device(source, z, x, c)).wait_recv()
    parts = [recv[i].astype(F32) for i in range(SIDE)]
    own = x * 2 + c
    xb[z, own] = jnp.concatenate([part[:CAP] for part in parts], axis=0).astype(BF16)
    sb[z, own] = jnp.concatenate([part[CAP:] for part in parts], axis=0).astype(BF16)

    partner = device(y, z, x, 1 - c)
    low, high = pl.ds(0, HALF), pl.ds(HALF, HALF)
    off = (0, 3, 1, 2)
    bufs = (xb, sb)

    def chunk(a, first, second):
        if a == 0:
            return xb.at[second, first * 2 + c]
        return sb.at[first, second * 2 + c]

    def mine(a):
        return (x, z) if a == 0 else (z, x)

    def first_dev(a, place_on):
        return device(y, z, place_on, c) if a == 0 else device(y, place_on, x, c)

    def second_dev(a, place_on):
        return device(y, place_on, x, c) if a == 0 else device(y, z, place_on, c)

    def to_partner(a, i, j):
        f, s = mine(a)
        ref = chunk(a, turn(f, off[j]), turn(s, off[i]))
        copy = remote(ref, ref, ps.at[a, i, j], pr.at[a, i, j], partner)
        copy.start()
        sends.append(copy)

    def from_partner(a, i, j):
        f, s = mine(a)
        first, second = turn(f, off[j]), turn(s, off[i])
        if a == 0:
            ref = xb.at[second, first * 2 + (1 - c)]
        else:
            ref = sb.at[first, second * 2 + (1 - c)]
        remote(ref, ref, ps.at[a, i, j], pr.at[a, i, j], partner).wait_recv()

    def first_send(a):
        f, s = mine(a)
        ref = chunk(a, f, s)
        for d, by in ((0, 1), (1, 3)):
            copy = remote(ref, ref, n1s.at[a, d], n1r.at[a, d], first_dev(a, turn(f, by)))
            copy.start()
            sends.append(copy)

    def first_recv(a, d):
        f, s = mine(a)
        source = turn(f, 3 if d == 0 else 1)
        ref = chunk(a, source, s)
        remote(ref, ref, n1s.at[a, d], n1r.at[a, d], first_dev(a, source)).wait_recv()
        part = ref.at[low if d == 0 else high]
        copy = remote(part, part, h1s.at[a, d], h1r.at[a, d], first_dev(a, turn(f, 1 if d == 0 else 3)))
        copy.start()
        sends.append(copy)

    def first_far(a):
        f, s = mine(a)
        ref = chunk(a, turn(f, 2), s)
        for d, part in ((0, ref.at[low]), (1, ref.at[high])):
            remote(part, part, h1s.at[a, d], h1r.at[a, d], first_dev(a, turn(f, 3 if d == 0 else 1))).wait_recv()

    def second_send(a, j):
        f, s = mine(a)
        ref = chunk(a, turn(f, off[j]), s)
        for d, by in ((0, 1), (1, 3)):
            copy = remote(ref, ref, n2s.at[a, j, d], n2r.at[a, j, d], second_dev(a, turn(s, by)))
            copy.start()
            sends.append(copy)

    def second_recv(a, j, d):
        f, s = mine(a)
        source = turn(s, 3 if d == 0 else 1)
        ref = chunk(a, turn(f, off[j]), source)
        remote(ref, ref, n2s.at[a, j, d], n2r.at[a, j, d], second_dev(a, source)).wait_recv()
        part = ref.at[low if d == 0 else high]
        copy = remote(part, part, h2s.at[a, j, d], h2r.at[a, j, d], second_dev(a, turn(s, 1 if d == 0 else 3)))
        copy.start()
        sends.append(copy)

    def second_far(a, j):
        f, s = mine(a)
        ref = chunk(a, turn(f, off[j]), turn(s, 2))
        for d, part in ((0, ref.at[low]), (1, ref.at[high])):
            remote(part, part, h2s.at[a, j, d], h2r.at[a, j, d], second_dev(a, turn(s, 3 if d == 0 else 1))).wait_recv()

    for a in (0, 1):
        first_send(a)
    for a in (0, 1):
        second_send(a, 0)
        to_partner(a, 0, 0)
    for d in (0, 1):
        for a in (0, 1):
            first_recv(a, d)
            second_send(a, 1 + d)
            to_partner(a, 0, 1 + d)
    for a in (0, 1):
        first_far(a)
        second_send(a, 3)
        to_partner(a, 0, 3)
    for j in range(SIDE):
        for d in (0, 1):
            for a in (0, 1):
                second_recv(a, j, d)
                to_partner(a, 1 + d, j)
        if j > 0:
            for a in (0, 1):
                second_far(a, j - 1)
                to_partner(a, 3, j - 1)
    for a in (0, 1):
        second_far(a, SIDE - 1)
        to_partner(a, 3, SIDE - 1)
    for a in (0, 1):
        for i in range(SIDE):
            for j in range(SIDE):
                from_partner(a, i, j)
    out_x = pltpu.make_async_copy(xb, xg, out_sem.at[0])
    out_s = pltpu.make_async_copy(sb, sg, out_sem.at[1])
    out_x.start()
    out_s.start()
    for load in loads:
        load.wait()
    acc_g[...] = jnp.zeros_like(acc_g)
    acc_u[...] = jnp.zeros_like(acc_u)
    acc_d[...] = jnp.zeros_like(acc_d)

    def step(k, carry):
        rows_x = xb[:, k].reshape(SIDE * ROWS, 512)
        rows_s = sb[:, k].reshape(SIDE * ROWS, 512)
        acc_g[...] += lax.dot_general(rows_x, wgv[k], NT, preferred_element_type=F32)
        acc_u[...] += lax.dot_general(rows_x, wuv[k], NT, preferred_element_type=F32)
        acc_d[...] += lax.dot_general(rows_s, wdv[k], NT, preferred_element_type=F32)
        return carry

    lax.fori_loop(0, KCH, step, 0)

    def activate(i, carry):
        rows = pl.ds(pl.multiple_of(i * 32, 32), 32)
        gate = acc_g[rows, :]
        up = acc_u[rows, :]
        d_hidden = acc_d[rows, :]
        squash = jax.nn.sigmoid(gate)
        active = gate * squash
        h_out[rows, :] = (active * up).astype(BF16)
        dg_out[rows, :] = (d_hidden * up * squash * (1.0 + gate * (1.0 - squash))).astype(BF16)
        du_out[rows, :] = (d_hidden * active).astype(BF16)
        return carry

    lax.fori_loop(0, SIDE * ROWS // 32, activate, 0)
    out_x.wait()
    out_s.wait()
    for copy in sends:
        copy.wait_send()


def grads_kernel(xg, sg, h, dg, du, gate_out, up_out, down_out, ht, dgt, dut):
    @pl.when(pl.program_id(0) == 0)
    def _():
        ht[...] = jnp.transpose(h[...])
        dgt[...] = jnp.transpose(dg[...])
        dut[...] = jnp.transpose(du[...])

    rows_x = xg[...].reshape(SIDE * ROWS, 512)
    rows_s = sg[...].reshape(SIDE * ROWS, 512)
    gate_out[...] = jnp.dot(dgt[...], rows_x, preferred_element_type=F32).astype(BF16)
    up_out[...] = jnp.dot(dut[...], rows_x, preferred_element_type=F32).astype(BF16)
    down_out[...] = jnp.dot(ht[...], rows_s, preferred_element_type=F32).astype(BF16)


def scatter_kernel(
    routes, probs, h, dg, du, wg, wu, wd, layer_out, token_out,
    wgv, wuv, wdv, own, psend, precv, far, farr, mid, midr, far2, far2r, mid2, mid2r, first_sum, ysend, yrecv,
    w_sem, ps, pr, fs, fr, ms, mr, f2s, f2r, m2s, m2r, ys, yr,
):
    y, z, x, c = place()
    for k in range(KCH):
        for i, (src, dst) in enumerate(((wg, wgv), (wu, wuv), (wd, wdv))):
            pltpu.make_async_copy(src.at[:, pl.ds(k * 512, 512)], dst.at[k], w_sem.at[i, k]).start()
    greet(y, z, x, c)
    partner = device(y, z, x, 1 - c)
    low, high = pl.ds(0, HALF), pl.ds(HALF, HALF)

    def offset(j):
        return lax.rem(2 + j + lax.div(j, 2) + 2 * lax.div(j, 3), SIDE)

    def first_dev(a, by):
        return device(y, turn(z, by), x, c) if a == 0 else device(y, z, turn(x, by), c)

    def second_dev(a, by):
        return device(y, z, turn(x, by), c) if a == 0 else device(y, turn(z, by), x, c)

    def partner_copy(a, j):
        return remote(psend.at[a, j], precv.at[a, j], ps.at[a, j], pr.at[a, j], partner)

    def compute(j):
        at = turn(x, offset(j))
        rows = h[...].reshape(SIDE * ROWS, 448)
        keep = jnp.dot(rows, wdv[at * 2 + c], preferred_element_type=F32)
        own[0, j] = keep.reshape(SIDE, ROWS, 512)
        give = jnp.dot(rows, wdv[at * 2 + 1 - c], preferred_element_type=F32)
        psend[0, j] = give.astype(BF16).reshape(SIDE, ROWS, 512)
        partner_copy(0, j).start()
        at = turn(z, offset(j))
        rows_g, rows_u = dg[at], du[at]

        def columns(i, carry):
            keep = jnp.dot(rows_g, wgv[i * 2 + c], preferred_element_type=F32)
            keep += jnp.dot(rows_u, wuv[i * 2 + c], preferred_element_type=F32)
            own[1, j, i] = keep
            give = jnp.dot(rows_g, wgv[i * 2 + 1 - c], preferred_element_type=F32)
            give += jnp.dot(rows_u, wuv[i * 2 + 1 - c], preferred_element_type=F32)
            psend[1, j, i] = give.astype(BF16)
            return carry

        lax.fori_loop(0, SIDE, columns, 0)
        partner_copy(1, j).start()

    def here(a):
        return z if a == 0 else x

    def pair_sum(a, j, by):
        at = turn(here(a), by)
        return own[a, j, at] + precv[a, j, at].astype(F32)

    def far_copy(a, j, d):
        part = high if d == 0 else low
        return remote(far.at[a, j, part], farr.at[a, j, d], fs.at[a, j, d], fr.at[a, j, d], first_dev(a, 1 if d == 0 else 3))

    def send_far(a, j):
        partner_copy(a, j).wait_recv()
        far[a, j] = pair_sum(a, j, 2).astype(BF16)
        far_copy(a, j, 0).start()
        far_copy(a, j, 1).start()

    def mid_copy(a, j, d):
        return remote(mid.at[a, j, d], midr.at[a, j, d], ms.at[a, j, d], mr.at[a, j, d], first_dev(a, 1 if d == 0 else 3))

    def send_mid(a, j):
        for d, by in ((0, 1), (1, 3)):
            total = pair_sum(a, j, by)
            far_copy(a, j, d).wait_recv()
            part = farr[a, j, d].astype(F32)
            if d == 0:
                total = jnp.concatenate([total[:HALF], total[HALF:] + part], axis=0)
            else:
                total = jnp.concatenate([total[:HALF] + part, total[HALF:]], axis=0)
            mid[a, j, d] = total.astype(BF16)
            mid_copy(a, j, d).start()

    def finish_first(a, j):
        total = pair_sum(a, j, 0)
        for d in (0, 1):
            mid_copy(a, j, d).wait_recv()
            total = total + midr[a, j, d].astype(F32)
        first_sum[a, j] = total

    def far2_copy(a, d):
        part = high if d == 0 else low
        return remote(far2.at[a, part], far2r.at[a, d], f2s.at[a, d], f2r.at[a, d], second_dev(a, 1 if d == 0 else 3))

    def mid2_copy(a, d):
        return remote(mid2.at[a, d], mid2r.at[a, d], m2s.at[a, d], m2r.at[a, d], second_dev(a, 1 if d == 0 else 3))

    def send_far2(a):
        far2[a] = first_sum[a, 0].astype(BF16)
        far2_copy(a, 0).start()
        far2_copy(a, 1).start()

    def send_mid2(a, d):
        total = first_sum[a, 2 if d == 0 else 1]
        far2_copy(a, d).wait_recv()
        part = far2r[a, d].astype(F32)
        if d == 0:
            total = jnp.concatenate([total[:HALF], total[HALF:] + part], axis=0)
        else:
            total = jnp.concatenate([total[:HALF] + part, total[HALF:]], axis=0)
        mid2[a, d] = total.astype(BF16)
        mid2_copy(a, d).start()

    def finish_second(a):
        total = first_sum[a, 3]
        for d in (0, 1):
            mid2_copy(a, d).wait_recv()
            total = total + mid2r[a, d].astype(F32)
        return total

    for i, (src, dst) in enumerate(((wg, wgv), (wu, wuv), (wd, wdv))):
        for k in range(KCH):
            pltpu.make_async_copy(src.at[:, pl.ds(k * 512, 512)], dst.at[k], w_sem.at[i, k]).wait()

    def pipeline(t, carry):
        @pl.when(t < SIDE)
        def _():
            compute(t)

        @pl.when((t >= 1) & (t <= SIDE))
        def _():
            send_far(0, t - 1)
            send_far(1, t - 1)

        @pl.when(t >= 2)
        def _():
            send_mid(0, t - 2)
            send_mid(1, t - 2)

        return carry

    lax.fori_loop(0, SIDE + 2, pipeline, 0)
    for a in (0, 1):
        finish_first(a, 0)
        send_far2(a)
    for a in (0, 1):
        finish_first(a, 1)
        send_mid2(a, 1)
    for a in (0, 1):
        finish_first(a, 2)
        send_mid2(a, 0)
    for a in (0, 1):
        finish_first(a, 3)
    totals = [finish_second(a) for a in (0, 1)]
    for i in range(SIDE):
        piece = [total[i * CAP:(i + 1) * CAP] for total in totals]
        ysend[i] = jnp.concatenate(piece, axis=0).astype(BF16)
    y_copies = []
    for by in (1, 2, 3):
        target = turn(y, by)
        copy = remote(ysend.at[target], yrecv.at[y], ys.at[by - 1], yr.at[by - 1], device(target, z, x, c))
        copy.start()
        y_copies.append(copy)
    yrecv[y] = ysend[y]

    count = layer_out.shape[0]
    route = routes[...]
    prob = probs[...]
    square = (count, count)
    first = lax.broadcasted_iota(jnp.int32, square, 0)
    second = lax.broadcasted_iota(jnp.int32, square, 1)
    before = jnp.where(second < first, 1.0, 0.0).astype(BF16)
    lane = lax.broadcasted_iota(jnp.int32, (count, 2 * CAP), 1).astype(F32)
    r0 = jnp.broadcast_to(route[:, 0:1], (count, 2 * CAP))
    r1 = jnp.broadcast_to(route[:, 1:2], (count, 2 * CAP))
    picks = []
    for e in range(EXP):
        member = jnp.where(r0 == e, 1.0, 0.0) + jnp.where(r1 == e, 1.0, 0.0)
        placed = jnp.dot(before, member.astype(BF16), preferred_element_type=F32)
        pick_out = jnp.where(placed == lane, member, 0.0).astype(BF16)
        pick_dx = jnp.where(placed + CAP == lane, member, 0.0).astype(BF16)
        pick_out = jnp.where(lane < CAP, pick_out.astype(F32), 0.0).astype(BF16)
        weight = jnp.where(route[:, 0:1] == e, prob[:, 0:1], 0.0) + jnp.where(route[:, 1:2] == e, prob[:, 1:2], 0.0)
        picks.append((pick_out, pick_dx, weight))
    for by in (1, 2, 3):
        source = turn(y, SIDE - by)
        remote(ysend.at[source], yrecv.at[source], ys.at[by - 1], yr.at[by - 1], device(source, z, x, c)).wait_recv()
    layer = jnp.zeros(layer_out.shape, F32)
    token = jnp.zeros(token_out.shape, F32)
    for e in range(EXP):
        pick_out, pick_dx, weight = picks[e]
        rows = yrecv[e]
        layer = layer + weight * jnp.dot(pick_out, rows, preferred_element_type=F32)
        token = token + jnp.dot(pick_dx, rows, preferred_element_type=F32)
    layer_out[...] = layer.astype(BF16)
    token_out[...] = token.astype(BF16)

    for copy in y_copies:
        copy.wait_send()
    for a in (0, 1):
        for d in (0, 1):
            far2_copy(a, d).wait_send()
            mid2_copy(a, d).wait_send()

    def drain(j, carry):
        for a in (0, 1):
            partner_copy(a, j).wait_send()
            for d in (0, 1):
                far_copy(a, j, d).wait_send()
                mid_copy(a, j, d).wait_send()
        return carry

    lax.fori_loop(0, SIDE, drain, 0)


def per_device(tokens, routes, route_probs, grad_out, w_gate, w_up, w_down):
    hidden_units, width = w_gate.shape
    rows = SIDE * ROWS
    vmem = pl.BlockSpec(memory_space=pltpu.VMEM)
    anywhere = pl.BlockSpec(memory_space=pl.ANY)
    dma = pltpu.SemaphoreType.DMA
    gathered = jax.ShapeDtypeStruct((SIDE, KCH, ROWS, 512), BF16)
    small = jax.ShapeDtypeStruct((rows, hidden_units), BF16)
    weight_buf = pltpu.VMEM((KCH, hidden_units, 512), BF16)
    xg, sg, h, dg, du = pl.pallas_call(
        gather_kernel,
        out_shape=(gathered, gathered, small, small, small),
        in_specs=[vmem] * 4 + [anywhere] * 3,
        out_specs=(anywhere, anywhere, vmem, vmem, vmem),
        scratch_shapes=[
            pltpu.VMEM((EXP, 2 * CAP, 512), BF16),
            pltpu.VMEM((SIDE, 2 * CAP, 512), BF16),
            pltpu.VMEM((SIDE, KCH, ROWS, 512), BF16),
            pltpu.VMEM((SIDE, KCH, ROWS, 512), BF16),
            weight_buf, weight_buf, weight_buf,
            pltpu.VMEM((rows, hidden_units), F32),
            pltpu.VMEM((rows, hidden_units), F32),
            pltpu.VMEM((rows, hidden_units), F32),
            dma((3, KCH)), dma((2,)), dma((3,)), dma((3,)),
            dma((2, 2)), dma((2, 2)), dma((2, 2)), dma((2, 2)),
            dma((2, 4, 2)), dma((2, 4, 2)), dma((2, 4, 2)), dma((2, 4, 2)),
            dma((2, 4, 4)), dma((2, 4, 4)),
        ],
        compiler_params=pltpu.CompilerParams(collective_id=0, has_side_effects=True, vmem_limit_bytes=VMEM_LIMIT),
        name="gather_rows",
    )(routes, route_probs, tokens, grad_out, w_gate, w_up, w_down)

    block = pl.BlockSpec((SIDE, 1, ROWS, 512), lambda k: (0, k, 0, 0))
    whole = pl.BlockSpec((rows, hidden_units), lambda k: (0, 0))
    grad_spec = pl.BlockSpec((hidden_units, 512), lambda k: (0, k))
    grad_shape = jax.ShapeDtypeStruct((hidden_units, width), BF16)
    grad_gate, grad_up, grad_down = pl.pallas_call(
        grads_kernel,
        grid=(KCH,),
        out_shape=(grad_shape,) * 3,
        in_specs=[block, block, whole, whole, whole],
        out_specs=(grad_spec,) * 3,
        scratch_shapes=[pltpu.VMEM((hidden_units, rows), BF16)] * 3,
        compiler_params=pltpu.CompilerParams(vmem_limit_bytes=VMEM_LIMIT),
        name="weight_grads",
    )(xg, sg, h, dg, du)

    stacked = (SIDE, ROWS, hidden_units)
    token_shape = jax.ShapeDtypeStruct(tokens.shape, BF16)
    layer_out, grad_tokens = pl.pallas_call(
        scatter_kernel,
        out_shape=(token_shape, token_shape),
        in_specs=[vmem] * 5 + [anywhere] * 3,
        out_specs=(vmem, vmem),
        scratch_shapes=[
            weight_buf, weight_buf, weight_buf,
            pltpu.VMEM((2, SIDE, SIDE, ROWS, 512), F32),
            pltpu.VMEM((2, SIDE, SIDE, ROWS, 512), BF16),
            pltpu.VMEM((2, SIDE, SIDE, ROWS, 512), BF16),
            pltpu.VMEM((2, SIDE, ROWS, 512), BF16),
            pltpu.VMEM((2, SIDE, 2, HALF, 512), BF16),
            pltpu.VMEM((2, SIDE, 2, ROWS, 512), BF16),
            pltpu.VMEM((2, SIDE, 2, ROWS, 512), BF16),
            pltpu.VMEM((2, ROWS, 512), BF16),
            pltpu.VMEM((2, 2, HALF, 512), BF16),
            pltpu.VMEM((2, 2, ROWS, 512), BF16),
            pltpu.VMEM((2, 2, ROWS, 512), BF16),
            pltpu.VMEM((2, SIDE, ROWS, 512), F32),
            pltpu.VMEM((SIDE, 2 * CAP, 512), BF16),
            pltpu.VMEM((SIDE, 2 * CAP, 512), BF16),
            dma((3, KCH)), dma((2, 4)), dma((2, 4)),
            dma((2, 4, 2)), dma((2, 4, 2)), dma((2, 4, 2)), dma((2, 4, 2)),
            dma((2, 2)), dma((2, 2)), dma((2, 2)), dma((2, 2)),
            dma((3,)), dma((3,)),
        ],
        compiler_params=pltpu.CompilerParams(collective_id=1, has_side_effects=True, vmem_limit_bytes=VMEM_LIMIT),
        name="scatter_sums",
    )(routes, route_probs, h.reshape(stacked), dg.reshape(stacked), du.reshape(stacked), w_gate, w_up, w_down)
    return layer_out, grad_tokens, grad_gate, grad_up, grad_down


def solution(mesh):
    return jax.shard_map(
        per_device,
        mesh=mesh,
        in_specs=(
            P("dp", "et"),
            P("dp", None),
            P("dp", None),
            P("dp", "et"),
            P(("dp", "et"), None),
            P(("dp", "et"), None),
            P(("dp", "et"), None),
        ),
        out_specs=(
            P("dp", "et"),
            P("dp", "et"),
            P(("dp", "et"), None),
            P(("dp", "et"), None),
            P(("dp", "et"), None),
        ),
        check_vma=False,
    )
```

time: 923 us -> 134 us (0.15)
  waiting for transfers between devices: 283 us -> 0 us
  blocking collectives: 201 us -> 0 us
  local copies, waits for them, and re-layouts: 199 us -> 5.96 us
  matrix products: 160 us -> 0 us
  Pallas kernels: 0 us -> 127 us
  other arithmetic: 32.6 us -> 0 us
  starting transfers between devices: 28.8 us -> 0 us
  between operations: 15.3 us -> 0.65 us
    all_to_all x3 -> x0, waiting for transfers between devices: 215 us -> none  [the longest x1 165 us: per_device(): lax.all_to_all(dx_rows, 'dp', split_axis=0, concat_axis=0, tiled=True)]
    dot_general x50 -> x0, matrix products: 160 us -> none  [the longest x5 49.1 us: one_tile(): lax.dot_general(d_up, tile_x, contract_first, preferred_element_type=jnp....]
    pallas_call x0 -> x3, Pallas kernels: none -> 127 us  [the longest x1 59.6 us: per_device(): pl.pallas_call(gather_kernel, out_shape=(gathered, gathered, small, small...]
    all_to_all x1 -> x0, blocking collectives: 119 us -> none  [per_device(): lax.all_to_all(out_rows, 'dp', split_axis=0, concat_axis=0, tiled=True)]
    scatter x10 -> x0, local copies, waits for them, and re-layouts: 101 us -> none  [the longest x5 52.8 us: one_tile(): dx_rows = dx_rows.at[row_index].set(dx_tile, mode='drop')]
    unnamed x1 -> x0, blocking collectives: 81.2 us -> none
    gather x10 -> x0, local copies, waits for them, and re-layouts: 53.7 us -> none  [the longest x5 26.8 us: one_tile(): tile_dy = jnp.take(flat_dy, row_index, axis=0, mode='fill', fill_value=0)]
    all_gather x2 -> x0, waiting for transfers between devices: 50.9 us -> none  [the longest x1 26.4 us: per_device(): lax.all_gather(tokens, 'et', axis=1, tiled=True)]
  transfers between devices with their start and end apart: 7 -> 0, of which waited for: 5 -> 0; matrix products, arithmetic and copies ran while one was open for 4% -> 0% of each run, Pallas kernels for 0% -> 0%
where the time goes in v1:
time: 134 us; the launch traced here: 133 us
  Pallas kernels  127 us (95%)
  local copies, waits for them, and re-layouts  5.96 us (4%)
    pallas_call x1, Pallas kernels, per_device(): pl.pallas_call(gather_kernel, out_shape=(gathered, gathered, small, small...  59.6 us
    pallas_call x1, Pallas kernels, per_device(): pl.pallas_call(scatter_kernel, out_shape=(token_shape, token_shape), in_s...  53.3 us
    pallas_call x1, Pallas kernels, per_device(): pl.pallas_call(grads_kernel, grid=(KCH,), out_shape=(grad_shape,) * 3, in...  14 us
    unnamed x4, local copies, waits for them, and re-layouts  5.96 us

profile of v1, /device:TPU:0, one launch (start us, length us, event | category | flops | bytes accessed | tf_op | source)
XLA Modules:
  0.0 133.5 jit_solution(217502128712858686)
XLA Ops:
  0.6 1.4 %copy.14.routes = s32[128,2]{1,0:T(8,128)} copy(s32[128,2]{0,1:T(2,128)} %param.8) | data formatting | bytes 2048 | tf_op args[1]
  2.0 1.4 %copy.15.probs = f32[128,2]{1,0:T(8,128)} copy(f32[128,2]{0,1:T(2,128)} %param.9) | data formatting | bytes 2048 | tf_op args[2]
  3.5 59.6 %gather_rows.1 = (bf16[4,8,160,512]{3,2,1,0:T(8,128)(2,1)}, bf16[4,8,160,512]{3,2,1,0:T(8,128)(2,1)}, bf16[640,448]{1,0:T(8,128)(2,1)}, bf16[640,448]{1,0:T(8,128)(2,1)}, bf16[640,448]{1,0:T(8,128)(2,1)}) custom-call(s32[128,2]{1,0:T(8,128)} %copy.14.routes, f32[128,2]{1,0:T(8,128)} %copy.15.probs, bf16[128,512]{1,0:T(8,128)(2,1)} %tok.1, ...), custom_call_target="tpu_custom_call" | custom-call | tf_op jit(solution)/shard_map/gather_rows/pallas_call | solution.py:499
  63.1 14.0 %weight_grads.1 = (bf16[448,4096]{1,0:T(8,128)(2,1)}, bf16[448,4096]{1,0:T(8,128)(2,1)}, bf16[448,4096]{1,0:T(8,128)(2,1)}) custom-call(bf16[4,8,160,512]{3,2,1,0:T(8,128)(2,1)} %get-tuple-element.20.xg, bf16[4,8,160,512]{3,2,1,0:T(8,128)(2,1)} %get-tuple-element.21.sg, bf16[640,448]{1,0:T(8,128)(2,1)} %get-tuple-element.15.h, ...), custom_call_target="tpu_custom_call" | custom-call | tf_op jit(solution)/shard_map/weight_grads/pallas_call | solution.py:526
  77.0 53.3 %scatter_sums.1 = (bf16[128,512]{1,0:T(8,128)(2,1)}, bf16[128,512]{1,0:T(8,128)(2,1)}) custom-call(s32[128,2]{1,0:T(8,128)} %copy.14.routes, f32[128,2]{1,0:T(8,128)} %copy.15.probs, bf16[4,160,448]{2,1,0:T(8,128)(2,1)} %bitcast.3, bf16[4,160,448]{2,1,0:T(8,128)(2,1)} %bitcast.4, bf16[4,160,448]{2,1,0:T(8,128)(2,1)} %bitcast.5, bf16[448,4096]{1,0:T(8,128)(2,1)} %wg.3, ...), custom_call_target="tpu_custom_call" | custom-call | tf_op jit(solution)/shard_map/scatter_sums/pallas_call | solution.py:539
  130.3 1.6 %copy.18 = bf16[128,512]{1,0:T(8,128)(2,1)} copy(bf16[128,512]{1,0:T(8,128)(2,1)} %get-tuple-element.30) | data formatting | bytes 262144
  131.9 1.6 %copy.19 = bf16[128,512]{1,0:T(8,128)(2,1)} copy(bf16[128,512]{1,0:T(8,128)(2,1)} %get-tuple-element.31) | data formatting | bytes 262144

commit v2 on v0

v2 whole, which is shorter than its diff:
```python
import jax
import jax.numpy as jnp
from jax import lax
from jax.experimental import pallas as pl
from jax.experimental.pallas import tpu as pltpu
from jax.sharding import PartitionSpec as P

MESH = pl.DeviceIdType.MESH
EXP = 4
CAP = 40
SIDE = 4
ROWS = SIDE * CAP
ALL_ROWS = SIDE * ROWS
HALF = ROWS // 2
ETS = 8
WIDE = 512
PART = 256
F32 = jnp.float32
BF16 = jnp.bfloat16
NT = (((1,), (1,)), ((), ()))
FLOWS = (0, 1)
VMEM_LIMIT = 60 * 1024 * 1024


def place():
    dp = lax.axis_index("dp")
    et = lax.axis_index("et")
    return lax.div(dp, SIDE), lax.rem(dp, SIDE), lax.div(et, 2), lax.rem(et, 2)


def turn(value, by):
    return lax.rem(value + by, SIDE)


def device(y, z, x, c):
    return (y * SIDE + z, x * 2 + c)


def remote(src, dst, send_sem, recv_sem, target):
    return pltpu.make_async_remote_copy(
        src_ref=src, dst_ref=dst, send_sem=send_sem, recv_sem=recv_sem, device_id=target, device_id_type=MESH
    )


def greet(y, z, x, c):
    barrier = pltpu.get_barrier_semaphore()
    others = [device(y, z, x, 1 - c)]
    others += [device(y, z, turn(x, 1), c), device(y, z, turn(x, 3), c)]
    others += [device(y, turn(z, 1), x, c), device(y, turn(z, 3), x, c)]
    others += [device(turn(y, by), z, x, c) for by in (1, 2, 3)]
    for other in others:
        pl.semaphore_signal(barrier, inc=1, device_id=other, device_id_type=MESH)
    pl.semaphore_wait(barrier, len(others))


def halves_below(value):
    return jnp.concatenate([value[:, :PART], value[:, PART:]], axis=0)


def pack_rows(routes, probs, tok, cot, pack):
    count = tok.shape[0]
    slots = (CAP, count)
    route = routes[...].astype(F32)
    prob = probs[...]
    r0 = jnp.broadcast_to(route[0:1], slots)
    r1 = jnp.broadcast_to(route[1:2], slots)
    p0 = jnp.broadcast_to(prob[0:1], slots)
    p1 = jnp.broadcast_to(prob[1:2], slots)
    square = (count, count)
    first = lax.broadcasted_iota(jnp.int32, square, 0)
    second = lax.broadcasted_iota(jnp.int32, square, 1)
    before = jnp.where(first < second, 1.0, 0.0).astype(BF16)
    slot = lax.broadcasted_iota(jnp.int32, slots, 0).astype(F32)
    x_all = tok[...]
    d_all = cot[...]
    for e in range(EXP):
        in0 = jnp.where(r0 == e, 1.0, 0.0)
        in1 = jnp.where(r1 == e, 1.0, 0.0)
        member = in0 + in1
        placed = jnp.dot(member.astype(BF16), before, preferred_element_type=F32)
        pick = jnp.where(placed == slot, member, 0.0)
        weight = jnp.sum(pick * (in0 * p0 + in1 * p1), axis=1, keepdims=True)
        pick = pick.astype(BF16)
        chosen = jnp.dot(pick, x_all, preferred_element_type=F32)
        scaled = weight * jnp.dot(pick, d_all, preferred_element_type=F32)
        pack[0, e] = halves_below(chosen).astype(BF16)
        pack[1, e] = halves_below(scaled).astype(BF16)


def main_kernel(
    routes, probs, tok, cot, wg, wu, wd, xg, sg, h_out, dg_out, du_out, back_out,
    pack, recv, xb, sb, wgv, wuv, wdv, acc_g, acc_u, acc_d, hb, dgb, dub,
    own, precv, far, farr, mid, midr, far2, far2r, mid2, mid2r, first_sum, ysend, yrecv,
    w_sem, out_sem, ys, yr, n1s, n1r, h1s, h1r, n2s, n2r, h2s, h2r, ps, pr,
    qs, qr, fs, fr, ms, mr, f2s, f2r, m2s, m2r, bs, br,
):
    y, z, x, c = place()
    for i, (src, dst) in enumerate(((wg, wgv), (wu, wuv), (wd, wdv))):
        for k in range(ETS):
            pltpu.make_async_copy(src.at[:, pl.ds(k * WIDE, WIDE)], dst.at[k], w_sem.at[i, k]).start()

    def weights_here(i):
        src, dst = ((wg, wgv), (wu, wuv), (wd, wdv))[i]
        for k in range(ETS):
            pltpu.make_async_copy(src.at[:, pl.ds(k * WIDE, WIDE)], dst.at[k], w_sem.at[i, k]).wait()

    pack_rows(routes, probs, tok, cot, pack)
    greet(y, z, x, c)

    def y_copy(a, by, slot_from, slot_to, target):
        return remote(pack.at[a, slot_from], recv.at[a, slot_to], ys.at[a, by - 1], yr.at[a, by - 1], device(target, z, x, c))

    for a in (0, 1):
        for by in (1, 2, 3):
            e = turn(y, by)
            y_copy(a, by, e, y, e).start()

    bufs = (xb, sb)
    own_et = x * 2 + c
    partner = device(y, z, x, 1 - c)
    low, high = pl.ds(0, HALF), pl.ds(HALF, HALF)

    def assemble(a):
        recv[a, y] = pack[a, y]
        for by in (1, 2, 3):
            source = turn(y, SIDE - by)
            y_copy(a, by, source, source, source).wait_recv()
        parts = [recv[a, i].astype(F32) for i in range(SIDE)]
        for h in FLOWS:
            piece = [part[h * CAP:(h + 1) * CAP] for part in parts]
            bufs[a][z, own_et * 2 + h] = jnp.concatenate(piece, axis=0).astype(BF16)

    def chunk(a, h, first, second, core):
        if h == 0:
            return bufs[a].at[second, (first * 2 + core) * 2]
        return bufs[a].at[first, (second * 2 + core) * 2 + 1]

    def mine(h):
        return (x, z) if h == 0 else (z, x)

    def on_x(by):
        return device(y, z, turn(x, by), c)

    def on_z(by):
        return device(y, turn(z, by), x, c)

    def first_dev(h, by):
        return on_x(by) if h == 0 else on_z(by)

    def second_dev(h, by):
        return on_z(by) if h == 0 else on_x(by)

    GO = (1, 3)
    COME = (3, 1)

    def swap_copy(a, h, i, j, core):
        f, s = mine(h)
        ref = chunk(a, h, turn(f, j), turn(s, i), core)
        return remote(ref, ref, ps.at[a, h, i, j], pr.at[a, h, i, j], partner)

    def to_partner(a, h, i, j):
        swap_copy(a, h, i, j, c).start()

    def from_partner(a):
        def one(n, carry):
            for h in FLOWS:
                swap_copy(a, h, lax.div(n, SIDE), lax.rem(n, SIDE), 1 - c).wait_recv()
            return carry

        lax.fori_loop(0, SIDE * SIDE, one, 0)

    def first_full(a, h, d, by):
        f, s = mine(h)
        ref = chunk(a, h, turn(f, by), s, c)
        return ref, remote(ref, ref, n1s.at[a, h, d], n1r.at[a, h, d], first_dev(h, GO[d]))

    def first_half(a, h, d, by):
        f, s = mine(h)
        ref = chunk(a, h, turn(f, by), s, c).at[low if d == 0 else high]
        return remote(ref, ref, h1s.at[a, h, d], h1r.at[a, h, d], first_dev(h, GO[d]))

    def second_full(a, h, j, d, by):
        f, s = mine(h)
        ref = chunk(a, h, turn(f, j), turn(s, by), c)
        return remote(ref, ref, n2s.at[a, h, j, d], n2r.at[a, h, j, d], second_dev(h, GO[d]))

    def second_half(a, h, j, d, by):
        f, s = mine(h)
        ref = chunk(a, h, turn(f, j), turn(s, by), c).at[low if d == 0 else high]
        return remote(ref, ref, h2s.at[a, h, j, d], h2r.at[a, h, j, d], second_dev(h, GO[d]))

    def first_send(a):
        for d in (0, 1):
            for h in FLOWS:
                first_full(a, h, d, 0)[1].start()

    def second_send(a, j):
        for d in (0, 1):
            for h in FLOWS:
                second_full(a, h, j, d, 0).start()
        for h in FLOWS:
            to_partner(a, h, 0, j)

    def first_recv(a, d):
        for h in FLOWS:
            first_full(a, h, d, COME[d])[1].wait_recv()
            first_half(a, h, d, COME[d]).start()
        second_send(a, COME[d])

    def first_far(a):
        for h in FLOWS:
            for d in (0, 1):
                first_half(a, h, d, 2).wait_recv()
        second_send(a, 2)

    def second_recv(a, j):
        for d in (0, 1):
            for h in FLOWS:
                second_full(a, h, j, d, COME[d]).wait_recv()
                second_half(a, h, j, d, COME[d]).start()
                to_partner(a, h, COME[d], j)

    def second_far(a, j):
        for h in FLOWS:
            for d in (0, 1):
                second_half(a, h, j, d, 2).wait_recv()
            to_partner(a, h, 2, j)

    def gather_sent(a):
        for h in FLOWS:
            for d in (0, 1):
                first_full(a, h, d, 0)[1].wait_send()
                first_half(a, h, d, COME[d]).wait_send()

            def one(n, carry, h=h):
                swap_copy(a, h, lax.div(n, SIDE), lax.rem(n, SIDE), c).wait_send()
                return carry

            lax.fori_loop(0, SIDE * SIDE, one, 0)

            def ring(j, carry, h=h):
                for d in (0, 1):
                    second_full(a, h, j, d, 0).wait_send()
                    second_half(a, h, j, d, COME[d]).wait_send()
                return carry

            lax.fori_loop(0, SIDE, ring, 0)

    def rows_of(buf, k):
        left = buf[:, k * 2].reshape(ALL_ROWS, PART)
        right = buf[:, k * 2 + 1].reshape(ALL_ROWS, PART)
        return jnp.concatenate([left, right], axis=1)

    def gate_up(k0, k1):
        def step(k, carry):
            rows = rows_of(xb, k)
            acc_g[...] += lax.dot_general(rows, wgv[k], NT, preferred_element_type=F32)
            acc_u[...] += lax.dot_general(rows, wuv[k], NT, preferred_element_type=F32)
            return carry

        lax.fori_loop(k0, k1, step, 0)

    def d_hidden(k0, k1):
        def step(k, carry):
            acc_d[...] += lax.dot_general(rows_of(sb, k), wdv[k], NT, preferred_element_type=F32)
            return carry

        lax.fori_loop(k0, k1, step, 0)

    def activate():
        def step(i, carry):
            rows = pl.ds(pl.multiple_of(i * 32, 32), 32)
            gate = acc_g[rows, :]
            up = acc_u[rows, :]
            squash = jax.nn.sigmoid(gate)
            active = gate * squash
            hb[rows, :] = (active * up).astype(BF16)
            acc_g[rows, :] = up * squash * (1.0 + gate * (1.0 - squash))
            acc_u[rows, :] = active
            return carry

        lax.fori_loop(0, ALL_ROWS // 32, step, 0)

    def activate_back():
        def step(i, carry):
            rows = pl.ds(pl.multiple_of(i * 32, 32), 32)
            back = acc_d[rows, :]
            dgb[rows, :] = (back * acc_g[rows, :]).astype(BF16)
            dub[rows, :] = (back * acc_u[rows, :]).astype(BF16)
            return carry

        lax.fori_loop(0, ALL_ROWS // 32, step, 0)

    def give(b, h, sl):
        return xb.at[sl, pl.ds((b * 2 + h) * SIDE, SIDE)]

    def pair_copy(b, h, j):
        sl = turn(x if h == 0 else z, j)
        return remote(give(b, h, sl), precv.at[b, h, sl], qs.at[b, h, j], qr.at[b, h, j], partner)

    def keep_and_give(b, j):
        at = turn(x, j)

        def product(core):
            if b == 0:
                return jnp.dot(hb[...], wdv[at * 2 + core], preferred_element_type=F32)
            out = jnp.dot(dgb[...], wgv[at * 2 + core], preferred_element_type=F32)
            return out + jnp.dot(dub[...], wuv[at * 2 + core], preferred_element_type=F32)

        stacked = (SIDE, ROWS, PART)
        other = product(1 - c).astype(BF16)
        xb[at, pl.ds(b * 2 * SIDE, SIDE)] = other[:, :PART].reshape(stacked)
        xb[:, (b * 2 + 1) * SIDE + at] = other[:, PART:].reshape(stacked)
        pair_copy(b, 0, j).start()
        keep = product(c)
        own[b, 0, at] = keep[:, :PART].reshape(stacked)
        own[b, 1, :, at] = keep[:, PART:].reshape(stacked)

    def give_rest(b):
        for j in (2, 3, 1, 0):
            pair_copy(b, 1, j).start()

    def ring1(h, by):
        return on_z(by) if h == 0 else on_x(by)

    def ring2(h, by):
        return on_x(by) if h == 0 else on_z(by)

    def pair_sum(b, h, j, by):
        sl = turn(x if h == 0 else z, j)
        fi = turn(z if h == 0 else x, by)
        return own[b, h, sl, fi] + precv[b, h, sl, fi].astype(F32)

    def far_copy(b, h, j, d):
        part = high if d == 0 else low
        return remote(far.at[b, h, j, part], farr.at[b, h, j, d], fs.at[b, h, j, d], fr.at[b, h, j, d], ring1(h, GO[d]))

    def send_far(b, h, j):
        pair_copy(b, h, j).wait_recv()
        far[b, h, j] = pair_sum(b, h, j, 2).astype(BF16)
        for d in (0, 1):
            far_copy(b, h, j, d).start()

    def mid_copy(b, h, j, d):
        return remote(mid.at[b, h, j, d], midr.at[b, h, j, d], ms.at[b, h, j, d], mr.at[b, h, j, d], ring1(h, GO[d]))

    def add_half(total, part, d):
        if d == 0:
            return jnp.concatenate([total[:HALF], total[HALF:] + part], axis=0)
        return jnp.concatenate([total[:HALF] + part, total[HALF:]], axis=0)

    def send_mid(b, j):
        for d in (0, 1):
            for h in FLOWS:
                total = pair_sum(b, h, j, GO[d])
                far_copy(b, h, j, d).wait_recv()
                total = add_half(total, farr[b, h, j, d].astype(F32), d)
                mid[b, h, j, d] = total.astype(BF16)
                mid_copy(b, h, j, d).start()

    def finish_first(b, h, j):
        total = pair_sum(b, h, j, 0)
        for d in (0, 1):
            mid_copy(b, h, j, d).wait_recv()
            total = total + midr[b, h, j, d].astype(F32)
        first_sum[b, h, j] = total

    def far2_copy(b, h, d):
        part = high if d == 0 else low
        return remote(far2.at[b, h, part], far2r.at[b, h, d], f2s.at[b, h, d], f2r.at[b, h, d], ring2(h, GO[d]))

    def mid2_copy(b, h, d):
        return remote(mid2.at[b, h, d], mid2r.at[b, h, d], m2s.at[b, h, d], m2r.at[b, h, d], ring2(h, GO[d]))

    def send_far2(b):
        for h in FLOWS:
            finish_first(b, h, 2)
            far2[b, h] = first_sum[b, h, 2].astype(BF16)
            for d in (0, 1):
                far2_copy(b, h, d).start()

    def send_mid2(b, d):
        for h in FLOWS:
            finish_first(b, h, GO[d])
            total = first_sum[b, h, GO[d]]
            far2_copy(b, h, d).wait_recv()
            total = add_half(total, far2r[b, h, d].astype(F32), d)
            mid2[b, h, d] = total.astype(BF16)
            mid2_copy(b, h, d).start()

    def back_copy(b, by, slot_from, slot_to, target):
        return remote(ysend.at[b, slot_from], yrecv.at[b, slot_to], bs.at[b, by - 1], br.at[b, by - 1], device(target, z, x, c))

    def send_back(b):
        totals = []
        for h in FLOWS:
            finish_first(b, h, 0)
            total = first_sum[b, h, 0]
            for d in (0, 1):
                mid2_copy(b, h, d).wait_recv()
                total = total + mid2r[b, h, d].astype(F32)
            totals.append(total)
        for i in range(SIDE):
            piece = [total[i * CAP:(i + 1) * CAP] for total in totals]
            ysend[b, i] = jnp.concatenate(piece, axis=0).astype(BF16)
        for by in (1, 2, 3):
            target = turn(y, by)
            back_copy(b, by, target, y, target).start()
        yrecv[b, y] = ysend[b, y]

    def back_here(b):
        for by in (1, 2, 3):
            source = turn(y, SIDE - by)
            back_copy(b, by, source, source, source).wait_recv()
        back_out[b] = yrecv[b]

    assemble(0)
    first_send(0)
    second_send(0, 0)
    acc_g[...] = jnp.zeros_like(acc_g)
    acc_u[...] = jnp.zeros_like(acc_u)
    acc_d[...] = jnp.zeros_like(acc_d)
    assemble(1)
    first_recv(0, 0)
    first_recv(0, 1)
    second_recv(0, 0)
    first_far(0)
    second_recv(0, 3)
    first_send(1)
    second_send(1, 0)
    second_far(0, 0)
    second_recv(0, 1)
    second_far(0, 3)
    second_recv(0, 2)
    second_far(0, 1)
    first_recv(1, 0)
    first_recv(1, 1)
    second_far(0, 2)
    from_partner(0)
    out_x = pltpu.make_async_copy(xb, xg, out_sem.at[0])
    out_x.start()
    weights_here(0)
    weights_here(1)
    gate_up(0, 2)
    second_recv(1, 0)
    first_far(1)
    gate_up(2, 5)
    second_recv(1, 3)
    second_far(1, 0)
    gate_up(5, 8)
    activate()
    second_recv(1, 1)
    second_far(1, 3)
    gather_sent(0)
    out_x.wait()
    weights_here(2)
    keep_and_give(0, 2)
    keep_and_give(0, 3)
    second_recv(1, 2)
    second_far(1, 1)
    send_far(0, 0, 2)
    keep_and_give(0, 1)
    send_far(0, 0, 3)
    keep_and_give(0, 0)
    give_rest(0)
    send_far(0, 0, 1)
    second_far(1, 2)
    send_far(0, 1, 2)
    send_far(0, 1, 3)
    send_far(0, 0, 0)
    send_far(0, 1, 1)
    send_far(0, 1, 0)
    from_partner(1)
    out_s = pltpu.make_async_copy(sb, sg, out_sem.at[1])
    out_s.start()
    d_hidden(0, 3)
    send_mid(0, 2)
    d_hidden(3, 6)
    send_mid(0, 3)
    d_hidden(6, 8)
    activate_back()
    send_mid(0, 1)
    keep_and_give(1, 2)
    send_mid(0, 0)
    keep_and_give(1, 3)
    send_far2(0)
    send_far(1, 0, 2)
    keep_and_give(1, 1)
    send_far(1, 0, 3)
    send_mid2(0, 1)
    keep_and_give(1, 0)
    give_rest(1)
    send_far(1, 0, 1)
    send_far(1, 1, 2)
    send_far(1, 1, 3)
    send_far(1, 0, 0)
    send_far(1, 1, 1)
    send_far(1, 1, 0)
    send_mid2(0, 0)
    h_out[...] = hb[...]
    dg_out[...] = dgb[...]
    du_out[...] = dub[...]
    send_mid(1, 2)
    send_mid(1, 3)
    send_back(0)
    send_mid(1, 1)
    send_mid(1, 0)
    send_far2(1)
    send_mid2(1, 1)
    send_mid2(1, 0)
    back_here(0)
    send_back(1)
    back_here(1)

    out_s.wait()
    gather_sent(1)
    for a in (0, 1):
        for by in (1, 2, 3):
            e = turn(y, by)
            y_copy(a, by, e, y, e).wait_send()
            back_copy(a, by, e, y, e).wait_send()
        for h in FLOWS:
            for d in (0, 1):
                far2_copy(a, h, d).wait_send()
                mid2_copy(a, h, d).wait_send()

            def drain(j, carry, a=a, h=h):
                pair_copy(a, h, j).wait_send()
                for d in (0, 1):
                    far_copy(a, h, j, d).wait_send()
                    mid_copy(a, h, j, d).wait_send()
                return carry

            lax.fori_loop(0, SIDE, drain, 0)


def spread_back(routes, probs, back, layer_out, token_out):
    count = layer_out.shape[0]
    square = (count, count)
    route = routes[...].astype(F32)
    prob = probs[...]
    r0 = jnp.transpose(jnp.broadcast_to(route[0:1], square))
    r1 = jnp.transpose(jnp.broadcast_to(route[1:2], square))
    p0 = jnp.transpose(jnp.broadcast_to(prob[0:1], square))[:, 0:1]
    p1 = jnp.transpose(jnp.broadcast_to(prob[1:2], square))[:, 0:1]
    first = lax.broadcasted_iota(jnp.int32, square, 0)
    second = lax.broadcasted_iota(jnp.int32, square, 1)
    before = jnp.where(second < first, 1.0, 0.0).astype(BF16)
    lane = second.astype(F32)
    layer = [jnp.zeros((count, PART), F32) for _ in FLOWS]
    token = [jnp.zeros((count, PART), F32) for _ in FLOWS]
    for e in range(EXP):
        in0 = jnp.where(r0 == e, 1.0, 0.0)
        in1 = jnp.where(r1 == e, 1.0, 0.0)
        member = in0 + in1
        placed = jnp.dot(before, member.astype(BF16), preferred_element_type=F32)
        weight = in0[:, 0:1] * p0 + in1[:, 0:1] * p1
        for h in FLOWS:
            pick = jnp.where(placed + h * CAP == lane, member, 0.0)
            pick = jnp.where((lane >= h * CAP) & (lane < (h + 1) * CAP), pick, 0.0)
            pick = pick[:, :2 * CAP].astype(BF16)
            layer[h] = layer[h] + weight * jnp.dot(pick, back[0, e], preferred_element_type=F32)
            token[h] = token[h] + jnp.dot(pick, back[1, e], preferred_element_type=F32)
    layer_out[...] = jnp.concatenate(layer, axis=1).astype(BF16)
    token_out[...] = jnp.concatenate(token, axis=1).astype(BF16)


def grads_kernel(
    routes, probs, back, xg, sg, h, dg, du, layer_out, token_out, gate_out, up_out, down_out, ht, dt
):
    units = gate_out.shape[0]

    @pl.when(pl.program_id(0) == 0)
    def _():
        ht[...] = jnp.transpose(h[...])
        dt[:units] = jnp.transpose(dg[...])
        dt[units:] = jnp.transpose(du[...])
        spread_back(routes, probs, back, layer_out, token_out)

    for i in FLOWS:
        columns = slice(i * PART, (i + 1) * PART)
        rows_x = xg[:, i].reshape(ALL_ROWS, PART)
        rows_s = sg[:, i].reshape(ALL_ROWS, PART)
        both = jnp.dot(dt[...], rows_x, preferred_element_type=F32).astype(BF16)
        gate_out[:, columns] = both[:units]
        up_out[:, columns] = both[units:]
        down_out[:, columns] = jnp.dot(ht[...], rows_s, preferred_element_type=F32).astype(BF16)


def per_device(tokens, routes, route_probs, grad_out, w_gate, w_up, w_down):
    units, width = w_gate.shape
    count = tokens.shape[0]
    vmem = pl.BlockSpec(memory_space=pltpu.VMEM)
    anywhere = pl.BlockSpec(memory_space=pl.ANY)
    dma = pltpu.SemaphoreType.DMA
    gathered = jax.ShapeDtypeStruct((SIDE, 2 * ETS, ROWS, PART), BF16)
    small = jax.ShapeDtypeStruct((ALL_ROWS, units), BF16)
    back_shape = jax.ShapeDtypeStruct((2, EXP, 2 * CAP, PART), BF16)
    weight_buf = pltpu.VMEM((ETS, units, WIDE), BF16)
    gather_buf = pltpu.VMEM((SIDE, 2 * ETS, ROWS, PART), BF16)
    acc = pltpu.VMEM((ALL_ROWS, units), F32)
    hidden_buf = pltpu.VMEM((ALL_ROWS, units), BF16)
    packed = pltpu.VMEM((2, EXP, 2 * CAP, PART), BF16)
    routes_t = routes.T
    probs_t = route_probs.T
    xg, sg, h, dg, du, back = pl.pallas_call(
        main_kernel,
        out_shape=(gathered, gathered, small, small, small, back_shape),
        in_specs=[vmem] * 4 + [anywhere] * 3,
        out_specs=(anywhere, anywhere, vmem, vmem, vmem, vmem),
        scratch_shapes=[
            packed, packed, gather_buf, gather_buf, weight_buf, weight_buf, weight_buf,
            acc, acc, acc, hidden_buf, hidden_buf, hidden_buf,
            pltpu.VMEM((2, 2, SIDE, SIDE, ROWS, PART), F32),
            pltpu.VMEM((2, 2, SIDE, SIDE, ROWS, PART), BF16),
            pltpu.VMEM((2, 2, SIDE, ROWS, PART), BF16),
            pltpu.VMEM((2, 2, SIDE, 2, HALF, PART), BF16),
            pltpu.VMEM((2, 2, SIDE, 2, ROWS, PART), BF16),
            pltpu.VMEM((2, 2, SIDE, 2, ROWS, PART), BF16),
            pltpu.VMEM((2, 2, ROWS, PART), BF16),
            pltpu.VMEM((2, 2, 2, HALF, PART), BF16),
            pltpu.VMEM((2, 2, 2, ROWS, PART), BF16),
            pltpu.VMEM((2, 2, 2, ROWS, PART), BF16),
            pltpu.VMEM((2, 2, SIDE, ROWS, PART), F32),
            packed, packed,
            dma((3, ETS)), dma((2,)), dma((2, 3)), dma((2, 3)),
            dma((2, 2, 2)), dma((2, 2, 2)), dma((2, 2, 2)), dma((2, 2, 2)),
            dma((2, 2, 4, 2)), dma((2, 2, 4, 2)), dma((2, 2, 4, 2)), dma((2, 2, 4, 2)),
            dma((2, 2, 4, 4)), dma((2, 2, 4, 4)),
            dma((2, 2, 4)), dma((2, 2, 4)),
            dma((2, 2, 4, 2)), dma((2, 2, 4, 2)), dma((2, 2, 4, 2)), dma((2, 2, 4, 2)),
            dma((2, 2, 2)), dma((2, 2, 2)), dma((2, 2, 2)), dma((2, 2, 2)),
            dma((2, 3)), dma((2, 3)),
        ],
        compiler_params=pltpu.CompilerParams(collective_id=0, has_side_effects=True, vmem_limit_bytes=VMEM_LIMIT),
        name="expert_layer",
    )(routes_t, probs_t, tokens, grad_out, w_gate, w_up, w_down)

    block = pl.BlockSpec((SIDE, 2, ROWS, PART), lambda k: (0, k, 0, 0))
    whole = pl.BlockSpec((ALL_ROWS, units), lambda k: (0, 0))
    route_spec = pl.BlockSpec(routes_t.shape, lambda k: (0, 0))
    token_spec = pl.BlockSpec(tokens.shape, lambda k: (0, 0))
    token_shape = jax.ShapeDtypeStruct(tokens.shape, BF16)
    grad_spec = pl.BlockSpec((units, WIDE), lambda k: (0, k))
    grad_shape = jax.ShapeDtypeStruct((units, width), BF16)
    return pl.pallas_call(
        grads_kernel,
        grid=(width // WIDE,),
        out_shape=(token_shape, token_shape, grad_shape, grad_shape, grad_shape),
        in_specs=[
            route_spec, route_spec, pl.BlockSpec(back_shape.shape, lambda k: (0, 0, 0, 0)),
            block, block, whole, whole, whole,
        ],
        out_specs=(token_spec, token_spec, grad_spec, grad_spec, grad_spec),
        scratch_shapes=[pltpu.VMEM((units, ALL_ROWS), BF16), pltpu.VMEM((2 * units, ALL_ROWS), BF16)],
        compiler_params=pltpu.CompilerParams(vmem_limit_bytes=VMEM_LIMIT),
        name="weight_grads",
    )(routes_t, probs_t, back, xg, sg, h, dg, du)


def solution(mesh):
    return jax.shard_map(
        per_device,
        mesh=mesh,
        in_specs=(
            P("dp", "et"),
            P("dp", None),
            P("dp", None),
            P("dp", "et"),
            P(("dp", "et"), None),
            P(("dp", "et"), None),
            P(("dp", "et"), None),
        ),
        out_specs=(
            P("dp", "et"),
            P("dp", "et"),
            P(("dp", "et"), None),
            P(("dp", "et"), None),
            P(("dp", "et"), None),
        ),
        check_vma=False,
    )
```

time: 923 us -> 115 us (0.12)
  waiting for transfers between devices: 283 us -> 0 us
  blocking collectives: 201 us -> 0 us
  local copies, waits for them, and re-layouts: 199 us -> 0 us
  matrix products: 160 us -> 0 us
  Pallas kernels: 0 us -> 114 us
  other arithmetic: 32.6 us -> 0 us
  starting transfers between devices: 28.8 us -> 0 us
  between operations: 15.3 us -> 0.64 us
    all_to_all x3 -> x0, waiting for transfers between devices: 215 us -> none  [the longest x1 165 us: per_device(): lax.all_to_all(dx_rows, 'dp', split_axis=0, concat_axis=0, tiled=True)]
    dot_general x50 -> x0, matrix products: 160 us -> none  [the longest x5 49.1 us: one_tile(): lax.dot_general(d_up, tile_x, contract_first, preferred_element_type=jnp....]
    all_to_all x1 -> x0, blocking collectives: 119 us -> none  [per_device(): lax.all_to_all(out_rows, 'dp', split_axis=0, concat_axis=0, tiled=True)]
    pallas_call x0 -> x2, Pallas kernels: none -> 114 us  [the longest x1 98.4 us: per_device(): pl.pallas_call(main_kernel, out_shape=(gathered, gathered, small, small,...]
    scatter x10 -> x0, local copies, waits for them, and re-layouts: 101 us -> none  [the longest x5 52.8 us: one_tile(): dx_rows = dx_rows.at[row_index].set(dx_tile, mode='drop')]
    unnamed x1 -> x0, blocking collectives: 81.2 us -> none
    gather x10 -> x0, local copies, waits for them, and re-layouts: 53.7 us -> none  [the longest x5 26.8 us: one_tile(): tile_dy = jnp.take(flat_dy, row_index, axis=0, mode='fill', fill_value=0)]
    all_gather x2 -> x0, waiting for transfers between devices: 50.9 us -> none  [the longest x1 26.4 us: per_device(): lax.all_gather(tokens, 'et', axis=1, tiled=True)]
  transfers between devices with their start and end apart: 7 -> 0, of which waited for: 5 -> 0; matrix products, arithmetic and copies ran while one was open for 4% -> 0% of each run, Pallas kernels for 0% -> 0%
where the time goes in v2:
time: 115 us
  Pallas kernels  114 us (99%)
    pallas_call x1, Pallas kernels, per_device(): pl.pallas_call(main_kernel, out_shape=(gathered, gathered, small, small,...  98.4 us
    pallas_call x1, Pallas kernels, per_device(): pl.pallas_call(grads_kernel, grid=(width // WIDE,), out_shape=(token_shap...  15.5 us

profile of v2, /device:TPU:0, one launch (start us, length us, event | category | flops | bytes accessed | tf_op | source)
XLA Modules:
  0.0 114.6 jit_solution(13304562274306958267)
XLA Ops:
  0.6 98.4 %expert_layer.1 = (bf16[4,16,160,256]{3,2,1,0:T(8,128)(2,1)}, bf16[4,16,160,256]{3,2,1,0:T(8,128)(2,1)}, bf16[640,448]{1,0:T(8,128)(2,1)}, bf16[640,448]{1,0:T(8...) custom-call(s32[2,128]{1,0:T(2,128)} %bitcast.2, f32[2,128]{1,0:T(2,128)} %bitcast.4, ...), custom_call_target="tpu_custom_call" | custom-call | tf_op jit(solution)/shard_map/expert_layer/pallas_call | solution.py:606
  99.1 15.5 %weight_grads.1 = (bf16[128,512]{1,0:T(8,128)(2,1)}, bf16[128,512]{1,0:T(8,128)(2,1)}, bf16[448,4096]{1,0:T(8,128)(2,1)}, bf16[448,4096]{1,0:T(8,128)(2,1)}, bf16[448,4096]{1,0:T(8,128)(2,1)}) custom-call(s32[2,128]{1,0:T(2,128)} %bitcast.3, f32[2,128]{1,0:T(2,128)} %bitcast.5, bf16[2,4,80,256]{3,2,1,0:T(8,128)(2,1)} %get-tuple-element.11.back, ...), custom_call_target="tpu_custom_call" | custom-call | tf_op jit(solution)/shard_map/weight_grads/pallas_call | solution.py:646

commit v3 on v2

v3 whole, which is shorter than its diff:
```python
import jax
import jax.numpy as jnp
from jax import lax
from jax.experimental import pallas as pl
from jax.experimental.pallas import tpu as pltpu
from jax.sharding import PartitionSpec as P

MESH = pl.DeviceIdType.MESH
EXP = 4
CAP = 40
SIDE = 4
ROWS = SIDE * CAP
ALL_ROWS = SIDE * ROWS
HALF = ROWS // 2
ETS = 8
WIDE = 512
PART = 256
F32 = jnp.float32
BF16 = jnp.bfloat16
NT = (((1,), (1,)), ((), ()))
FLOWS = (0, 1)
VMEM_LIMIT = 62 * 1024 * 1024


def place():
    dp = lax.axis_index("dp")
    et = lax.axis_index("et")
    return lax.div(dp, SIDE), lax.rem(dp, SIDE), lax.div(et, 2), lax.rem(et, 2)


def turn(value, by):
    return lax.rem(value + by, SIDE)


def device(y, z, x, c):
    return (y * SIDE + z, x * 2 + c)


def remote(src, dst, send_sem, recv_sem, target):
    return pltpu.make_async_remote_copy(
        src_ref=src, dst_ref=dst, send_sem=send_sem, recv_sem=recv_sem, device_id=target, device_id_type=MESH
    )


def greet(y, z, x, c):
    barrier = pltpu.get_barrier_semaphore()
    others = [device(y, z, x, 1 - c)]
    others += [device(y, z, turn(x, 1), c), device(y, z, turn(x, 3), c)]
    others += [device(y, turn(z, 1), x, c), device(y, turn(z, 3), x, c)]
    others += [device(turn(y, by), z, x, c) for by in (1, 2, 3)]
    for other in others:
        pl.semaphore_signal(barrier, inc=1, device_id=other, device_id_type=MESH)
    pl.semaphore_wait(barrier, len(others))


def halves_below(value):
    return jnp.concatenate([value[:, :PART], value[:, PART:]], axis=0)


def pack_rows(routes, probs, tok, cot, pack):
    count = tok.shape[0]
    slots = (CAP, count)
    route = routes[...].astype(F32)
    prob = probs[...]
    r0 = jnp.broadcast_to(route[0:1], slots)
    r1 = jnp.broadcast_to(route[1:2], slots)
    p0 = jnp.broadcast_to(prob[0:1], slots)
    p1 = jnp.broadcast_to(prob[1:2], slots)
    square = (count, count)
    first = lax.broadcasted_iota(jnp.int32, square, 0)
    second = lax.broadcasted_iota(jnp.int32, square, 1)
    before = jnp.where(first < second, 1.0, 0.0).astype(BF16)
    slot = lax.broadcasted_iota(jnp.int32, slots, 0).astype(F32)
    x_all = tok[...]
    d_all = cot[...]
    for e in range(EXP):
        in0 = jnp.where(r0 == e, 1.0, 0.0)
        in1 = jnp.where(r1 == e, 1.0, 0.0)
        member = in0 + in1
        placed = jnp.dot(member.astype(BF16), before, preferred_element_type=F32)
        pick = jnp.where(placed == slot, member, 0.0)
        weight = jnp.sum(pick * (in0 * p0 + in1 * p1), axis=1, keepdims=True)
        pick = pick.astype(BF16)
        chosen = jnp.dot(pick, x_all, preferred_element_type=F32)
        scaled = weight * jnp.dot(pick, d_all, preferred_element_type=F32)
        pack[0, e] = halves_below(chosen).astype(BF16)
        pack[1, e] = halves_below(scaled).astype(BF16)


def main_kernel(
    routes, probs, tok, cot, wg, wu, wd, gate_out, up_out, down_out, back_out,
    pack, recv, xb, sb, wgv, wuv, wdv, acc_g, acc_u, acc_d, hb, dgb, dub,
    own, psend, precv, far, farr, mid, midr, far2, far2r, mid2, mid2r, ysend, yrecv, ht, dt, stage_x, stage_s,
    w_sem, out_sem, ys, yr, n1r, h1r, n2r, h2r, ring_s, ps, pr, qs, qr, fr, mr, f2r, m2r, sum_s, bs, br,
):
    y, z, x, c = place()
    weights = ((wg, wgv), (wu, wuv), (wd, wdv))
    for i, (src, dst) in enumerate(weights):
        for k in range(ETS):
            pltpu.make_async_copy(src.at[:, pl.ds(k * WIDE, WIDE)], dst.at[k], w_sem.at[i]).start()

    def wait_bytes(ref, sem):
        pltpu.make_async_copy(ref, ref, sem).wait()

    pack_rows(routes, probs, tok, cot, pack)
    greet(y, z, x, c)

    for a in (0, 1):
        for by in (1, 2, 3):
            e = turn(y, by)
            remote(pack.at[a, e], recv.at[a, y], ys.at[a], yr.at[a], device(e, z, x, c)).start()

    bufs = (xb, sb)
    own_et = x * 2 + c
    partner = device(y, z, x, 1 - c)
    low, high = pl.ds(0, HALF), pl.ds(HALF, HALF)
    three = pl.ds(0, 3)

    def assemble(a):
        recv[a, y] = pack[a, y]
        wait_bytes(recv.at[a, three], yr.at[a])
        parts = [recv[a, i].astype(F32) for i in range(SIDE)]
        for h in FLOWS:
            piece = [part[h * CAP:(h + 1) * CAP] for part in parts]
            bufs[a][z, own_et * 2 + h] = jnp.concatenate(piece, axis=0).astype(BF16)

    def chunk(a, h, first, second):
        if h == 0:
            return bufs[a].at[second, (first * 2 + c) * 2]
        return bufs[a].at[first, (second * 2 + c) * 2 + 1]

    def mine(h):
        return (x, z) if h == 0 else (z, x)

    def on_x(by):
        return device(y, z, turn(x, by), c)

    def on_z(by):
        return device(y, turn(z, by), x, c)

    def first_dev(h, by):
        return on_x(by) if h == 0 else on_z(by)

    def second_dev(h, by):
        return on_z(by) if h == 0 else on_x(by)

    GO = (1, 3)
    COME = (3, 1)
    one_chunk = xb.at[0, 0]
    two_chunks = xb.at[0, pl.ds(0, 2)]

    def to_partner(a, h, i, j):
        f, s = mine(h)
        ref = chunk(a, h, turn(f, j), turn(s, i))
        remote(ref, ref, ps.at[a], pr.at[a], partner).start()

    def from_partner(a):
        wait_bytes(bufs[a].at[:, pl.ds(0, ETS)], pr.at[a])

    def first_send(a, h):
        f, s = mine(h)
        ref = chunk(a, h, f, s)
        for d in (0, 1):
            remote(ref, ref, ring_s.at[a], n1r.at[a, h], first_dev(h, GO[d])).start()

    def second_send(a, h, j):
        f, s = mine(h)
        ref = chunk(a, h, turn(f, j), s)
        for d in (0, 1):
            remote(ref, ref, ring_s.at[a], n2r.at[a, h, j], second_dev(h, GO[d])).start()
        to_partner(a, h, 0, j)

    def first_recv(a, h):
        f, s = mine(h)
        wait_bytes(two_chunks, n1r.at[a, h])
        for d in (0, 1):
            ref = chunk(a, h, turn(f, COME[d]), s).at[low if d == 0 else high]
            remote(ref, ref, ring_s.at[a], h1r.at[a, h], first_dev(h, GO[d])).start()
        second_send(a, h, 1)
        second_send(a, h, 3)

    def first_far(a, h):
        wait_bytes(one_chunk, h1r.at[a, h])
        second_send(a, h, 2)

    def second_recv(a, h, j):
        f, s = mine(h)
        wait_bytes(two_chunks, n2r.at[a, h, j])
        for d in (0, 1):
            ref = chunk(a, h, turn(f, j), turn(s, COME[d])).at[low if d == 0 else high]
            remote(ref, ref, ring_s.at[a], h2r.at[a, h, j], second_dev(h, GO[d])).start()
        for d in (0, 1):
            to_partner(a, h, COME[d], j)

    def second_far(a, h, j):
        wait_bytes(one_chunk, h2r.at[a, h, j])
        to_partner(a, h, 2, j)

    def rows_of(buf, k):
        left = buf[:, k * 2].reshape(ALL_ROWS, PART)
        right = buf[:, k * 2 + 1].reshape(ALL_ROWS, PART)
        return jnp.concatenate([left, right], axis=1)

    def gate_ready():
        wait_bytes(wgv, w_sem.at[0])
        wait_bytes(wuv, w_sem.at[1])
        wait_bytes(wdv, w_sem.at[2])

    def add_to(acc, value, k):
        if k == 0:
            acc[...] = value
        else:
            acc[...] += value

    def gate_up(k):
        rows = rows_of(xb, k)
        add_to(acc_g, lax.dot_general(rows, wgv[k], NT, preferred_element_type=F32), k)
        add_to(acc_u, lax.dot_general(rows, wuv[k], NT, preferred_element_type=F32), k)

    def d_hidden(k):
        add_to(acc_d, lax.dot_general(rows_of(sb, k), wdv[k], NT, preferred_element_type=F32), k)

    STEPS = ALL_ROWS // 64

    def activate(part):
        def step(i, carry):
            rows = pl.ds(pl.multiple_of(i * 32, 32), 32)
            gate = acc_g[rows, :]
            up = acc_u[rows, :]
            squash = jax.nn.sigmoid(gate)
            active = gate * squash
            hb[rows, :] = (active * up).astype(BF16)
            acc_g[rows, :] = up * squash * (1.0 + gate * (1.0 - squash))
            acc_u[rows, :] = active
            return carry

        lax.fori_loop(part * STEPS, (part + 1) * STEPS, step, 0)

    def activate_back(part):
        def step(i, carry):
            rows = pl.ds(pl.multiple_of(i * 32, 32), 32)
            back = acc_d[rows, :]
            dgb[rows, :] = (back * acc_g[rows, :]).astype(BF16)
            dub[rows, :] = (back * acc_u[rows, :]).astype(BF16)
            return carry

        lax.fori_loop(part * STEPS, (part + 1) * STEPS, step, 0)

    stacked = (SIDE, ROWS, PART)

    def give_ready(b):
        if b == 1:
            wait_bytes(psend, qs)

    def send_pair(b, h, j):
        sl = turn(x if h == 0 else z, j)
        remote(psend.at[h, sl], precv.at[b, h, sl], qs, qr.at[b, h, j], partner).start()

    def product(b, et):
        if b == 0:
            return jnp.dot(hb[...], wdv[et], preferred_element_type=F32)
        out = jnp.dot(dgb[...], wgv[et], preferred_element_type=F32)
        return out + jnp.dot(dub[...], wuv[et], preferred_element_type=F32)

    def give(b, j):
        at = turn(x, j)
        other = product(b, at * 2 + 1 - c).astype(BF16)
        psend[0, at] = other[:, :PART].reshape(stacked)
        psend[1, :, at] = other[:, PART:].reshape(stacked)
        send_pair(b, 0, j)

    def keep(b, j):
        at = turn(x, j)
        value = product(b, at * 2 + c)
        own[b, 0, at] = value[:, :PART].reshape(stacked)
        own[b, 1, :, at] = value[:, PART:].reshape(stacked)

    def give_rest(b):
        for j in (2, 3, 1, 0):
            send_pair(b, 1, j)

    def ring1(h, by):
        return on_z(by) if h == 0 else on_x(by)

    def ring2(h, by):
        return on_x(by) if h == 0 else on_z(by)

    def spot(h, j, by):
        return turn(x if h == 0 else z, j), turn(z if h == 0 else x, by)

    def pair_sum(b, h, j, by):
        sl, fi = spot(h, j, by)
        return own[b, h, sl, fi] + precv[b, h, sl, fi].astype(F32)

    def send_far(b, h, j):
        sl, fi = spot(h, j, 2)
        wait_bytes(precv.at[b, h, sl], qr.at[b, h, j])
        far[b, h, j] = pair_sum(b, h, j, 2).astype(BF16)
        for d, part in ((0, high), (1, low)):
            remote(far.at[b, h, j, part], farr.at[b, h, j, d], sum_s.at[b], fr.at[b, h, j], ring1(h, GO[d])).start()

    def add_half(total, part, d):
        if d == 0:
            return jnp.concatenate([total[:HALF], total[HALF:] + part], axis=0)
        return jnp.concatenate([total[:HALF] + part, total[HALF:]], axis=0)

    def send_mid(b, h, j):
        wait_bytes(farr.at[b, h, j], fr.at[b, h, j])
        for d in (0, 1):
            total = add_half(pair_sum(b, h, j, GO[d]), farr[b, h, j, d].astype(F32), d)
            mid[b, h, j, d] = total.astype(BF16)
            remote(mid.at[b, h, j, d], midr.at[b, h, j, d], sum_s.at[b], mr.at[b, h, j], ring1(h, GO[d])).start()

    def finish_first(b, h, j):
        wait_bytes(midr.at[b, h, j], mr.at[b, h, j])
        sl, fi = spot(h, j, 0)
        total = pair_sum(b, h, j, 0)
        own[b, h, sl, fi] = total + midr[b, h, j, 0].astype(F32) + midr[b, h, j, 1].astype(F32)

    def first_sum(b, h, j):
        sl, fi = spot(h, j, 0)
        return own[b, h, sl, fi]

    def send_far2(b, h):
        far2[b, h] = first_sum(b, h, 2).astype(BF16)
        for d, part in ((0, high), (1, low)):
            remote(far2.at[b, h, part], far2r.at[b, h, d], sum_s.at[b], f2r.at[b, h], ring2(h, GO[d])).start()

    def send_mid2(b, h):
        wait_bytes(far2r.at[b, h], f2r.at[b, h])
        for d in (0, 1):
            total = add_half(first_sum(b, h, GO[d]), far2r[b, h, d].astype(F32), d)
            mid2[b, h, d] = total.astype(BF16)
            remote(mid2.at[b, h, d], mid2r.at[b, h, d], sum_s.at[b], m2r.at[b, h], ring2(h, GO[d])).start()

    def send_back(b):
        totals = []
        for h in FLOWS:
            wait_bytes(mid2r.at[b, h], m2r.at[b, h])
            total = first_sum(b, h, 0) + mid2r[b, h, 0].astype(F32) + mid2r[b, h, 1].astype(F32)
            totals.append(total)
        for i in range(SIDE):
            piece = [total[i * CAP:(i + 1) * CAP] for total in totals]
            ysend[b, i] = jnp.concatenate(piece, axis=0).astype(BF16)
        for by in (1, 2, 3):
            target = turn(y, by)
            remote(ysend.at[b, target], yrecv.at[b, y], bs.at[b], br.at[b], device(target, z, x, c)).start()
        yrecv[b, y] = ysend[b, y]

    def back_here(b):
        wait_bytes(yrecv.at[b, three], br.at[b])
        back_out[b] = yrecv[b]

    UNITS = wg.shape[0]

    def grads_ready():
        ht[...] = jnp.transpose(hb[...])
        dt[pl.ds(0, UNITS), :] = jnp.transpose(dgb[...])
        dt[pl.ds(UNITS, UNITS), :] = jnp.transpose(dub[...])

    def grad_copy(k, i):
        columns = pl.ds(k * WIDE, WIDE)
        slot = k % 2
        src = stage_s.at[slot] if i == 2 else stage_x.at[slot, pl.ds(i * UNITS, UNITS)]
        dst = (gate_out, up_out, down_out)[i]
        return pltpu.make_async_copy(src, dst.at[:, columns], out_sem.at[i, slot])

    def grad_x(k):
        if k > 1:
            grad_copy(k - 2, 0).wait()
            grad_copy(k - 2, 1).wait()
        stage_x[k % 2] = jnp.dot(dt[...], rows_of(xb, k), preferred_element_type=F32).astype(BF16)
        grad_copy(k, 0).start()
        grad_copy(k, 1).start()

    def grad_s(k):
        if k > 1:
            grad_copy(k - 2, 2).wait()
        stage_s[k % 2] = jnp.dot(ht[...], rows_of(sb, k), preferred_element_type=F32).astype(BF16)
        grad_copy(k, 2).start()

    assemble(0)
    first_send(0, 1)
    first_send(0, 0)
    second_send(0, 0, 0)
    second_send(0, 1, 0)
    assemble(1)
    first_recv(0, 1)
    first_recv(0, 0)
    second_recv(0, 0, 0)
    second_recv(0, 1, 0)
    first_far(0, 1)
    second_recv(0, 1, 1)
    second_recv(0, 0, 1)
    second_recv(0, 1, 3)
    second_recv(0, 0, 3)
    first_far(0, 0)
    second_far(0, 0, 0)
    second_far(0, 1, 0)
    second_far(0, 0, 1)
    second_far(0, 0, 3)
    second_recv(0, 1, 2)
    second_far(0, 1, 1)
    second_recv(0, 0, 2)
    second_far(0, 1, 3)
    first_send(1, 0)
    first_send(1, 1)
    second_send(1, 0, 0)
    second_send(1, 1, 0)
    second_far(0, 1, 2)
    second_far(0, 0, 2)
    first_recv(1, 0)
    from_partner(0)
    gate_ready()
    first_recv(1, 1)
    gate_up(0)
    second_recv(1, 1, 0)
    gate_up(1)
    first_far(1, 0)
    second_recv(1, 0, 0)
    gate_up(2)
    gate_up(3)
    second_recv(1, 1, 1)
    second_recv(1, 0, 1)
    gate_up(4)
    gate_up(5)
    second_recv(1, 0, 3)
    first_far(1, 1)
    second_recv(1, 1, 3)
    second_far(1, 1, 0)
    gate_up(6)
    second_far(1, 1, 1)
    gate_up(7)
    second_recv(1, 0, 2)
    activate(0)
    second_far(1, 0, 0)
    activate(1)
    second_recv(1, 1, 2)
    second_far(1, 0, 1)
    give_ready(0)
    give(0, 2)
    second_far(1, 1, 3)
    keep(0, 2)
    second_far(1, 0, 3)
    give(0, 3)
    keep(0, 3)
    second_far(1, 0, 2)
    second_far(1, 1, 2)
    give(0, 1)
    send_far(0, 0, 2)
    keep(0, 1)
    give(0, 0)
    send_far(0, 0, 3)
    keep(0, 0)
    from_partner(1)
    give_rest(0)
    send_far(0, 0, 1)
    send_mid(0, 0, 2)
    send_far(0, 0, 0)
    d_hidden(0)
    send_mid(0, 0, 3)
    send_far(0, 1, 2)
    d_hidden(1)
    send_far(0, 1, 3)
    send_mid(0, 0, 1)
    send_far(0, 1, 1)
    send_far(0, 1, 0)
    d_hidden(2)
    d_hidden(3)
    finish_first(0, 0, 2)
    send_far2(0, 0)
    send_mid(0, 1, 2)
    send_mid(0, 1, 3)
    send_mid(0, 0, 0)
    d_hidden(4)
    send_mid(0, 1, 1)
    d_hidden(5)
    send_mid(0, 1, 0)
    finish_first(0, 0, 3)
    d_hidden(6)
    d_hidden(7)
    activate_back(0)
    activate_back(1)
    finish_first(0, 0, 1)
    send_mid2(0, 0)
    give_ready(1)
    give(1, 2)
    finish_first(0, 1, 2)
    send_far2(0, 1)
    keep(1, 2)
    finish_first(0, 0, 0)
    finish_first(0, 1, 3)
    give(1, 3)
    send_far(1, 0, 2)
    keep(1, 3)
    finish_first(0, 1, 1)
    send_mid2(0, 1)
    give(1, 1)
    send_mid(1, 0, 2)
    send_far(1, 0, 3)
    finish_first(0, 1, 0)
    keep(1, 1)
    give(1, 0)
    send_far(1, 0, 1)
    send_back(0)
    keep(1, 0)
    give_rest(1)
    finish_first(1, 0, 2)
    send_far2(1, 0)
    send_far(1, 0, 0)
    grads_ready()
    send_mid(1, 0, 3)
    send_far(1, 1, 2)
    back_here(0)
    send_far(1, 1, 3)
    send_far(1, 1, 1)
    send_mid(1, 0, 0)
    send_far(1, 1, 0)
    send_mid(1, 0, 1)
    grad_x(0)
    send_mid(1, 1, 2)
    send_mid(1, 1, 3)
    finish_first(1, 0, 3)
    grad_s(0)
    send_mid(1, 1, 1)
    grad_x(1)
    send_mid(1, 1, 0)
    finish_first(1, 0, 0)
    grad_s(1)
    finish_first(1, 0, 1)
    send_mid2(1, 0)
    finish_first(1, 1, 2)
    send_far2(1, 1)
    grad_x(2)
    grad_s(2)
    finish_first(1, 1, 3)
    grad_x(3)
    grad_s(3)
    finish_first(1, 1, 1)
    send_mid2(1, 1)
    grad_x(4)
    finish_first(1, 1, 0)
    grad_s(4)
    grad_x(5)
    grad_s(5)
    send_back(1)
    grad_x(6)
    grad_s(6)
    grad_x(7)
    grad_s(7)
    back_here(1)

    for k in (ETS - 2, ETS - 1):
        for i in range(3):
            grad_copy(k, i).wait()
    wait_bytes(psend, qs)
    for a in (0, 1):
        wait_bytes(pack.at[a, three], ys.at[a])
        wait_bytes(ysend.at[a, three], bs.at[a])
        wait_bytes(bufs[a].at[:, pl.ds(0, ETS)], ps.at[a])
        thirty = bufs[a].at[pl.ds(0, 2), pl.ds(0, 15)]
        wait_bytes(thirty, ring_s.at[a])
        wait_bytes(thirty, sum_s.at[a])


def spread_back(routes, probs, back, layer_out, token_out):
    count = layer_out.shape[0]
    square = (count, count)
    route = routes[...].astype(F32)
    prob = probs[...]
    r0 = jnp.transpose(jnp.broadcast_to(route[0:1], square))
    r1 = jnp.transpose(jnp.broadcast_to(route[1:2], square))
    p0 = jnp.transpose(jnp.broadcast_to(prob[0:1], square))[:, 0:1]
    p1 = jnp.transpose(jnp.broadcast_to(prob[1:2], square))[:, 0:1]
    first = lax.broadcasted_iota(jnp.int32, square, 0)
    second = lax.broadcasted_iota(jnp.int32, square, 1)
    before = jnp.where(second < first, 1.0, 0.0).astype(BF16)
    lane = second.astype(F32)
    layer = [jnp.zeros((count, PART), F32) for _ in FLOWS]
    token = [jnp.zeros((count, PART), F32) for _ in FLOWS]
    for e in range(EXP):
        in0 = jnp.where(r0 == e, 1.0, 0.0)
        in1 = jnp.where(r1 == e, 1.0, 0.0)
        member = in0 + in1
        placed = jnp.dot(before, member.astype(BF16), preferred_element_type=F32)
        weight = in0[:, 0:1] * p0 + in1[:, 0:1] * p1
        for h in FLOWS:
            pick = jnp.where(placed + h * CAP == lane, member, 0.0)
            pick = jnp.where((lane >= h * CAP) & (lane < (h + 1) * CAP), pick, 0.0)
            pick = pick[:, :2 * CAP].astype(BF16)
            layer[h] = layer[h] + weight * jnp.dot(pick, back[0, e], preferred_element_type=F32)
            token[h] = token[h] + jnp.dot(pick, back[1, e], preferred_element_type=F32)
    layer_out[...] = jnp.concatenate(layer, axis=1).astype(BF16)
    token_out[...] = jnp.concatenate(token, axis=1).astype(BF16)


def finish_kernel(routes, probs, back, gate_in, up_in, down_in, layer_out, token_out, gate_out, up_out, down_out, held, sem):
    pairs = ((gate_in, gate_out), (up_in, up_out), (down_in, down_out))
    blocks = 4
    rows = gate_in.shape[0] // blocks

    def move(i, k, way):
        part = pl.ds(k * rows, rows)
        src, dst = pairs[i]
        if way == 0:
            return pltpu.make_async_copy(src.at[part], held.at[i, part], sem.at[0, i, k])
        return pltpu.make_async_copy(held.at[i, part], dst.at[part], sem.at[1, i, k])

    steps = [(i, k) for i in range(3) for k in range(blocks)]
    for i, k in steps:
        move(i, k, 0).start()
    spread_back(routes, probs, back, layer_out, token_out)
    for i, k in steps:
        move(i, k, 0).wait()
        move(i, k, 1).start()
    for i, k in steps:
        move(i, k, 1).wait()


def per_device(tokens, routes, route_probs, grad_out, w_gate, w_up, w_down):
    units, width = w_gate.shape
    count = tokens.shape[0]
    vmem = pl.BlockSpec(memory_space=pltpu.VMEM)
    anywhere = pl.BlockSpec(memory_space=pl.ANY)
    dma = pltpu.SemaphoreType.DMA
    back_shape = jax.ShapeDtypeStruct((2, EXP, 2 * CAP, PART), BF16)
    weight_buf = pltpu.VMEM((ETS, units, WIDE), BF16)
    gather_buf = pltpu.VMEM((SIDE, 2 * ETS, ROWS, PART), BF16)
    acc = pltpu.VMEM((ALL_ROWS, units), F32)
    hidden_buf = pltpu.VMEM((ALL_ROWS, units), BF16)
    packed = pltpu.VMEM((2, EXP, 2 * CAP, PART), BF16)
    routes_t = routes.T
    probs_t = route_probs.T
    grad_shape = jax.ShapeDtypeStruct((units, width), BF16)
    gate, up, down, back = pl.pallas_call(
        main_kernel,
        out_shape=(grad_shape, grad_shape, grad_shape, back_shape),
        in_specs=[vmem] * 4 + [anywhere] * 3,
        out_specs=(anywhere, anywhere, anywhere, vmem),
        scratch_shapes=[
            packed, packed, gather_buf, gather_buf, weight_buf, weight_buf, weight_buf,
            acc, acc, acc, hidden_buf, hidden_buf, hidden_buf,
            pltpu.VMEM((2, 2, SIDE, SIDE, ROWS, PART), F32),
            pltpu.VMEM((2, SIDE, SIDE, ROWS, PART), BF16),
            pltpu.VMEM((2, 2, SIDE, SIDE, ROWS, PART), BF16),
            pltpu.VMEM((2, 2, SIDE, ROWS, PART), BF16),
            pltpu.VMEM((2, 2, SIDE, 2, HALF, PART), BF16),
            pltpu.VMEM((2, 2, SIDE, 2, ROWS, PART), BF16),
            pltpu.VMEM((2, 2, SIDE, 2, ROWS, PART), BF16),
            pltpu.VMEM((2, 2, ROWS, PART), BF16),
            pltpu.VMEM((2, 2, 2, HALF, PART), BF16),
            pltpu.VMEM((2, 2, 2, ROWS, PART), BF16),
            pltpu.VMEM((2, 2, 2, ROWS, PART), BF16),
            packed, packed,
            pltpu.VMEM((units, ALL_ROWS), BF16),
            pltpu.VMEM((2 * units, ALL_ROWS), BF16),
            pltpu.VMEM((2, 2 * units, WIDE), BF16),
            pltpu.VMEM((2, units, WIDE), BF16),
            dma((3,)), dma((3, 2)), dma((2,)), dma((2,)),
            dma((2, 2)), dma((2, 2)), dma((2, 2, 4)), dma((2, 2, 4)), dma((2,)), dma((2,)), dma((2,)),
            dma(()), dma((2, 2, 4)), dma((2, 2, 4)), dma((2, 2, 4)), dma((2, 2)), dma((2, 2)), dma((2,)),
            dma((2,)), dma((2,)),
        ],
        compiler_params=pltpu.CompilerParams(collective_id=0, has_side_effects=True, vmem_limit_bytes=VMEM_LIMIT),
        name="expert_layer",
    )(routes_t, probs_t, tokens, grad_out, w_gate, w_up, w_down)

    token_shape = jax.ShapeDtypeStruct(tokens.shape, BF16)
    return pl.pallas_call(
        finish_kernel,
        out_shape=(token_shape, token_shape, grad_shape, grad_shape, grad_shape),
        in_specs=[vmem] * 3 + [anywhere] * 3,
        out_specs=(vmem, vmem, anywhere, anywhere, anywhere),
        scratch_shapes=[pltpu.VMEM((3, units, width), BF16), dma((2, 3, 4))],
        compiler_params=pltpu.CompilerParams(vmem_limit_bytes=VMEM_LIMIT),
        name="finish",
    )(routes_t, probs_t, back, gate, up, down)


def solution(mesh):
    return jax.shard_map(
        per_device,
        mesh=mesh,
        in_specs=(
            P("dp", "et"),
            P("dp", None),
            P("dp", None),
            P("dp", "et"),
            P(("dp", "et"), None),
            P(("dp", "et"), None),
            P(("dp", "et"), None),
        ),
        out_specs=(
            P("dp", "et"),
            P("dp", "et"),
            P(("dp", "et"), None),
            P(("dp", "et"), None),
            P(("dp", "et"), None),
        ),
        check_vma=False,
    )
```

time: 115 us -> 109 us (0.948)
  Pallas kernels: 114 us -> 108 us
    pallas_call x2, Pallas kernels: 114 us -> 108 us  [the longest x1 98.1 us: per_device(): pl.pallas_call(main_kernel, out_shape=(grad_shape, grad_shape, grad_shape...]
where the time goes in v3:
time: 109 us
  Pallas kernels  108 us (99%)
    pallas_call x1, Pallas kernels, per_device(): pl.pallas_call(main_kernel, out_shape=(grad_shape, grad_shape, grad_shape...  98.1 us
    pallas_call x1, Pallas kernels, per_device(): pl.pallas_call(finish_kernel, out_shape=(token_shape, token_shape, grad_s...  10.3 us

profile of v3, /device:TPU:0, one launch (start us, length us, event | category | flops | bytes accessed | tf_op | source)
XLA Modules:
  0.0 109.2 jit_solution(13239481289413286654)
XLA Ops:
  0.6 98.1 %expert_layer.1 = (bf16[448,4096]{1,0:T(8,128)(2,1)}, bf16[448,4096]{1,0:T(8,128)(2,1)}, bf16[448,4096]{1,0:T(8,128)(2,1)}, bf16[2,4,80,256]{3,2,1,0:T(8,128)(2,1)}) custom-call(s32[2,128]{1,0:T(2,128)} %bitcast.2, f32[2,128]{1,0:T(2,128)} %bitcast.4, bf16[128,512]{1,0:T(8,128)(2,1)} %tok.1, bf16[128,512]{1,0:T(8,128)(2,1)} %cot.1, bf16[448,4096]{1,0:T(8,128)(2,1)} %wg.1, ...), custom_call_target="tpu_custom_call" | custom-call | tf_op jit(solution)/shard_map/expert_layer/pallas_call | solution.py:635
  98.7 10.3 %finish.1 = (bf16[128,512]{1,0:T(8,128)(2,1)}, bf16[128,512]{1,0:T(8,128)(2,1)}, bf16[448,4096]{1,0:T(8,128)(2,1)}, bf16[448,4096]{1,0:T(8,128)(2,1)}, bf16[448,4096]{1,0:T(8,128)(2,1)}) custom-call(s32[2,128]{1,0:T(2,128)} %bitcast.3, f32[2,128]{1,0:T(2,128)} %bitcast.5, bf16[2,4,80,256]{3,2,1,0:T(8,128)(2,1)} %get-tuple-element.9.back, ...), custom_call_target="tpu_custom_call" | custom-call | tf_op jit(solution)/shard_map/finish/pallas_call | solution.py:669

commit v4 on v3

--- a/solution.py
+++ b/solution.py
@@ -50,7 +50,7 @@
     others += [device(turn(y, by), z, x, c) for by in (1, 2, 3)]
     for other in others:
         pl.semaphore_signal(barrier, inc=1, device_id=other, device_id_type=MESH)
-    pl.semaphore_wait(barrier, len(others))
+    return lambda: pl.semaphore_wait(barrier, len(others))
 
 
 def halves_below(value):
@@ -102,8 +102,9 @@
     def wait_bytes(ref, sem):
         pltpu.make_async_copy(ref, ref, sem).wait()
 
+    await_greetings = greet(y, z, x, c)
     pack_rows(routes, probs, tok, cot, pack)
-    greet(y, z, x, c)
+    await_greetings()
 
     for a in (0, 1):
         for by in (1, 2, 3):
@@ -152,10 +153,10 @@
     def to_partner(a, h, i, j):
         f, s = mine(h)
         ref = chunk(a, h, turn(f, j), turn(s, i))
-        remote(ref, ref, ps.at[a], pr.at[a], partner).start()
-
-    def from_partner(a):
-        wait_bytes(bufs[a].at[:, pl.ds(0, ETS)], pr.at[a])
+        remote(ref, ref, ps.at[a], pr.at[a, j if h == 0 else i], partner).start()
+
+    def from_partner(a, group):
+        wait_bytes(bufs[a].at[0, pl.ds(0, ETS)], pr.at[a, group])
 
     def first_send(a, h):
         f, s = mine(h)
@@ -206,19 +207,23 @@
         wait_bytes(wuv, w_sem.at[1])
         wait_bytes(wdv, w_sem.at[2])
 
-    def add_to(acc, value, k):
-        if k == 0:
+    def add_to(acc, value, first):
+        if first:
             acc[...] = value
         else:
             acc[...] += value
 
-    def gate_up(k):
+    def gate_up(group, core):
+        k = turn(x, group) * 2 + core
+        first = group == 0 and core == 0
         rows = rows_of(xb, k)
-        add_to(acc_g, lax.dot_general(rows, wgv[k], NT, preferred_element_type=F32), k)
-        add_to(acc_u, lax.dot_general(rows, wuv[k], NT, preferred_element_type=F32), k)
-
-    def d_hidden(k):
-        add_to(acc_d, lax.dot_general(rows_of(sb, k), wdv[k], NT, preferred_element_type=F32), k)
+        add_to(acc_g, lax.dot_general(rows, wgv[k], NT, preferred_element_type=F32), first)
+        add_to(acc_u, lax.dot_general(rows, wuv[k], NT, preferred_element_type=F32), first)
+
+    def d_hidden(group, core):
+        k = turn(x, group) * 2 + core
+        first = group == 0 and core == 0
+        add_to(acc_d, lax.dot_general(rows_of(sb, k), wdv[k], NT, preferred_element_type=F32), first)
 
     STEPS = ALL_ROWS // 64
 
@@ -384,6 +389,7 @@
     first_send(0, 0)
     second_send(0, 0, 0)
     second_send(0, 1, 0)
+    gate_ready()
     assemble(1)
     first_recv(0, 1)
     first_recv(0, 0)
@@ -397,156 +403,161 @@
     first_far(0, 0)
     second_far(0, 0, 0)
     second_far(0, 1, 0)
-    second_far(0, 0, 1)
-    second_far(0, 0, 3)
-    second_recv(0, 1, 2)
-    second_far(0, 1, 1)
-    second_recv(0, 0, 2)
-    second_far(0, 1, 3)
     first_send(1, 0)
     first_send(1, 1)
     second_send(1, 0, 0)
     second_send(1, 1, 0)
+    second_far(0, 0, 1)
+    second_recv(0, 1, 2)
+    second_far(0, 0, 3)
+    from_partner(0, 0)
+    gate_up(0, 0)
+    second_far(0, 1, 1)
+    gate_up(0, 1)
+    second_recv(0, 0, 2)
+    second_far(0, 1, 3)
+    from_partner(0, 1)
+    gate_up(1, 0)
+    first_recv(1, 0)
+    first_recv(1, 1)
+    from_partner(0, 3)
+    gate_up(1, 1)
+    second_recv(1, 1, 0)
+    second_recv(1, 0, 0)
+    gate_up(3, 0)
+    second_far(0, 0, 2)
     second_far(0, 1, 2)
-    second_far(0, 0, 2)
-    first_recv(1, 0)
-    from_partner(0)
-    gate_ready()
-    first_recv(1, 1)
-    gate_up(0)
-    second_recv(1, 1, 0)
-    gate_up(1)
+    gate_up(3, 1)
     first_far(1, 0)
-    second_recv(1, 0, 0)
-    gate_up(2)
-    gate_up(3)
+    second_recv(1, 0, 1)
     second_recv(1, 1, 1)
-    second_recv(1, 0, 1)
-    gate_up(4)
-    gate_up(5)
+    from_partner(0, 2)
+    gate_up(2, 0)
     second_recv(1, 0, 3)
+    gate_up(2, 1)
     first_far(1, 1)
     second_recv(1, 1, 3)
     second_far(1, 1, 0)
-    gate_up(6)
-    second_far(1, 1, 1)
-    gate_up(7)
-    second_recv(1, 0, 2)
     activate(0)
     second_far(1, 0, 0)
     activate(1)
-    second_recv(1, 1, 2)
-    second_far(1, 0, 1)
+    second_far(1, 1, 1)
     give_ready(0)
     give(0, 2)
-    second_far(1, 1, 3)
     keep(0, 2)
-    second_far(1, 0, 3)
+    second_recv(1, 0, 2)
     give(0, 3)
     keep(0, 3)
+    second_far(1, 0, 1)
+    from_partner(1, 0)
+    d_hidden(0, 0)
+    second_recv(1, 1, 2)
+    second_far(1, 0, 3)
+    d_hidden(0, 1)
+    second_far(1, 1, 3)
+    send_far(0, 0, 2)
+    give(0, 1)
     second_far(1, 0, 2)
+    keep(0, 1)
+    send_far(0, 0, 3)
+    give(0, 0)
+    keep(0, 0)
+    from_partner(1, 1)
+    from_partner(1, 3)
     second_far(1, 1, 2)
-    give(0, 1)
-    send_far(0, 0, 2)
-    keep(0, 1)
-    give(0, 0)
-    send_far(0, 0, 3)
-    keep(0, 0)
-    from_partner(1)
     give_rest(0)
+    d_hidden(1, 0)
+    d_hidden(1, 1)
     send_far(0, 0, 1)
     send_mid(0, 0, 2)
+    d_hidden(3, 0)
     send_far(0, 0, 0)
-    d_hidden(0)
     send_mid(0, 0, 3)
+    from_partner(1, 2)
+    d_hidden(3, 1)
     send_far(0, 1, 2)
-    d_hidden(1)
     send_far(0, 1, 3)
+    d_hidden(2, 0)
+    send_far(0, 1, 1)
     send_mid(0, 0, 1)
-    send_far(0, 1, 1)
     send_far(0, 1, 0)
-    d_hidden(2)
-    d_hidden(3)
+    d_hidden(2, 1)
+    activate_back(0)
+    activate_back(1)
+    give_ready(1)
+    give(1, 2)
+    send_mid(0, 1, 2)
     finish_first(0, 0, 2)
     send_far2(0, 0)
-    send_mid(0, 1, 2)
+    send_mid(0, 0, 0)
     send_mid(0, 1, 3)
-    send_mid(0, 0, 0)
-    d_hidden(4)
     send_mid(0, 1, 1)
-    d_hidden(5)
+    keep(1, 2)
+    finish_first(0, 0, 3)
+    send_far(1, 0, 2)
     send_mid(0, 1, 0)
-    finish_first(0, 0, 3)
-    d_hidden(6)
-    d_hidden(7)
-    activate_back(0)
-    activate_back(1)
+    give(1, 3)
     finish_first(0, 0, 1)
-    send_mid2(0, 0)
-    give_ready(1)
-    give(1, 2)
+    keep(1, 3)
     finish_first(0, 1, 2)
     send_far2(0, 1)
-    keep(1, 2)
+    send_mid2(0, 0)
+    give(1, 1)
     finish_first(0, 0, 0)
+    keep(1, 1)
     finish_first(0, 1, 3)
-    give(1, 3)
-    send_far(1, 0, 2)
-    keep(1, 3)
+    send_mid(1, 0, 2)
+    send_far(1, 0, 3)
+    give(1, 0)
+    keep(1, 0)
     finish_first(0, 1, 1)
     send_mid2(0, 1)
-    give(1, 1)
-    send_mid(1, 0, 2)
-    send_far(1, 0, 3)
+    send_far(1, 0, 1)
+    give_rest(1)
+    grads_ready()
     finish_first(0, 1, 0)
-    keep(1, 1)
-    give(1, 0)
-    send_far(1, 0, 1)
-    send_back(0)
-    keep(1, 0)
-    give_rest(1)
+    send_far(1, 0, 0)
     finish_first(1, 0, 2)
     send_far2(1, 0)
-    send_far(1, 0, 0)
-    grads_ready()
+    grad_x(0)
+    send_far(1, 1, 2)
     send_mid(1, 0, 3)
-    send_far(1, 1, 2)
-    back_here(0)
     send_far(1, 1, 3)
     send_far(1, 1, 1)
+    send_back(0)
+    send_far(1, 1, 0)
+    grad_s(0)
+    send_mid(1, 0, 1)
+    grad_x(1)
+    send_mid(1, 1, 2)
     send_mid(1, 0, 0)
-    send_far(1, 1, 0)
-    send_mid(1, 0, 1)
-    grad_x(0)
-    send_mid(1, 1, 2)
     send_mid(1, 1, 3)
     finish_first(1, 0, 3)
-    grad_s(0)
+    grad_s(1)
     send_mid(1, 1, 1)
-    grad_x(1)
+    back_here(0)
+    grad_x(2)
+    finish_first(1, 0, 1)
     send_mid(1, 1, 0)
-    finish_first(1, 0, 0)
-    grad_s(1)
-    finish_first(1, 0, 1)
     send_mid2(1, 0)
+    grad_s(2)
     finish_first(1, 1, 2)
     send_far2(1, 1)
-    grad_x(2)
-    grad_s(2)
+    finish_first(1, 0, 0)
+    grad_x(3)
     finish_first(1, 1, 3)
-    grad_x(3)
     grad_s(3)
+    grad_x(4)
+    grad_s(4)
     finish_first(1, 1, 1)
     send_mid2(1, 1)
-    grad_x(4)
+    grad_x(5)
     finish_first(1, 1, 0)
-    grad_s(4)
-    grad_x(5)
     grad_s(5)
-    send_back(1)
     grad_x(6)
     grad_s(6)
     grad_x(7)
+    send_back(1)
     grad_s(7)
     back_here(1)
 
@@ -609,10 +620,10 @@
     steps = [(i, k) for i in range(3) for k in range(blocks)]
     for i, k in steps:
         move(i, k, 0).start()
-    spread_back(routes, probs, back, layer_out, token_out)
     for i, k in steps:
         move(i, k, 0).wait()
         move(i, k, 1).start()
+    spread_back(routes, probs, back, layer_out, token_out)
     for i, k in steps:
         move(i, k, 1).wait()
 
@@ -657,7 +668,7 @@
             pltpu.VMEM((2, 2 * units, WIDE), BF16),
             pltpu.VMEM((2, units, WIDE), BF16),
             dma((3,)), dma((3, 2)), dma((2,)), dma((2,)),
-            dma((2, 2)), dma((2, 2)), dma((2, 2, 4)), dma((2, 2, 4)), dma((2,)), dma((2,)), dma((2,)),
+            dma((2, 2)), dma((2, 2)), dma((2, 2, 4)), dma((2, 2, 4)), dma((2,)), dma((2,)), dma((2, 4)),
             dma(()), dma((2, 2, 4)), dma((2, 2, 4)), dma((2, 2, 4)), dma((2, 2)), dma((2, 2)), dma((2,)),
             dma((2,)), dma((2,)),
         ],

time: 109 us -> 100 us (0.917)
  Pallas kernels: 108 us -> 99 us
    pallas_call x1, Pallas kernels: 98.1 us -> 88.6 us  [per_device(): pl.pallas_call(main_kernel, out_shape=(grad_shape, grad_shape, grad_shape...]
where the time goes in v4:
time: 100 us; the launch traced here: 99.8 us
  Pallas kernels  99 us (99%)
    pallas_call x1, Pallas kernels, per_device(): pl.pallas_call(main_kernel, out_shape=(grad_shape, grad_shape, grad_shape...  88.6 us
    pallas_call x1, Pallas kernels, per_device(): pl.pallas_call(finish_kernel, out_shape=(token_shape, token_shape, grad_s...  10.4 us

profile of v4, /device:TPU:0, one launch (start us, length us, event | category | flops | bytes accessed | tf_op | source)
XLA Modules:
  0.0 99.8 jit_solution(10002270239778093673)
XLA Ops:
  0.6 88.6 %expert_layer.1 = (bf16[448,4096]{1,0:T(8,128)(2,1)}, bf16[448,4096]{1,0:T(8,128)(2,1)}, bf16[448,4096]{1,0:T(8,128)(2,1)}, bf16[2,4,80,256]{3,2,1,0:T(8,128)(2,1)}) custom-call(s32[2,128]{1,0:T(2,128)} %bitcast.2, f32[2,128]{1,0:T(2,128)} %bitcast.4, bf16[128,512]{1,0:T(8,128)(2,1)} %tok.1, bf16[128,512]{1,0:T(8,128)(2,1)} %cot.1, bf16[448,4096]{1,0:T(8,128)(2,1)} %wg.1, ...), custom_call_target="tpu_custom_call" | custom-call | tf_op jit(solution)/shard_map/expert_layer/pallas_call | solution.py:646
  89.3 10.4 %finish.1 = (bf16[128,512]{1,0:T(8,128)(2,1)}, bf16[128,512]{1,0:T(8,128)(2,1)}, bf16[448,4096]{1,0:T(8,128)(2,1)}, bf16[448,4096]{1,0:T(8,128)(2,1)}, bf16[448,4096]{1,0:T(8,128)(2,1)}) custom-call(s32[2,128]{1,0:T(2,128)} %bitcast.3, f32[2,128]{1,0:T(2,128)} %bitcast.5, bf16[2,4,80,256]{3,2,1,0:T(8,128)(2,1)} %get-tuple-element.9.back, ...), custom_call_target="tpu_custom_call" | custom-call | tf_op jit(solution)/shard_map/finish/pallas_call | solution.py:680

commit v5 on v4

--- a/solution.py
+++ b/solution.py
@@ -257,9 +257,8 @@
         if b == 1:
             wait_bytes(psend, qs)
 
-    def send_pair(b, h, j):
-        sl = turn(x if h == 0 else z, j)
-        remote(psend.at[h, sl], precv.at[b, h, sl], qs, qr.at[b, h, j], partner).start()
+    def pair_here(b, j):
+        wait_bytes(precv.at[b, turn(x, j)], qr.at[b, j])
 
     def product(b, et):
         if b == 0:
@@ -270,19 +269,15 @@
     def give(b, j):
         at = turn(x, j)
         other = product(b, at * 2 + 1 - c).astype(BF16)
-        psend[0, at] = other[:, :PART].reshape(stacked)
-        psend[1, :, at] = other[:, PART:].reshape(stacked)
-        send_pair(b, 0, j)
+        psend[at, 0] = other[:, :PART].reshape(stacked)
+        psend[at, 1] = other[:, PART:].reshape(stacked)
+        remote(psend.at[at], precv.at[b, at], qs, qr.at[b, j], partner).start()
 
     def keep(b, j):
         at = turn(x, j)
         value = product(b, at * 2 + c)
-        own[b, 0, at] = value[:, :PART].reshape(stacked)
-        own[b, 1, :, at] = value[:, PART:].reshape(stacked)
-
-    def give_rest(b):
-        for j in (2, 3, 1, 0):
-            send_pair(b, 1, j)
+        own[b, at, 0] = value[:, :PART].reshape(stacked)
+        own[b, at, 1] = value[:, PART:].reshape(stacked)
 
     def ring1(h, by):
         return on_z(by) if h == 0 else on_x(by)
@@ -291,15 +286,13 @@
         return on_x(by) if h == 0 else on_z(by)
 
     def spot(h, j, by):
-        return turn(x if h == 0 else z, j), turn(z if h == 0 else x, by)
+        return (turn(x, j), turn(z, by)) if h == 0 else (turn(x, by), turn(z, j))
 
     def pair_sum(b, h, j, by):
-        sl, fi = spot(h, j, by)
-        return own[b, h, sl, fi] + precv[b, h, sl, fi].astype(F32)
+        xx, zz = spot(h, j, by)
+        return own[b, xx, h, zz] + precv[b, xx, h, zz].astype(F32)
 
     def send_far(b, h, j):
-        sl, fi = spot(h, j, 2)
-        wait_bytes(precv.at[b, h, sl], qr.at[b, h, j])
         far[b, h, j] = pair_sum(b, h, j, 2).astype(BF16)
         for d, part in ((0, high), (1, low)):
             remote(far.at[b, h, j, part], farr.at[b, h, j, d], sum_s.at[b], fr.at[b, h, j], ring1(h, GO[d])).start()
@@ -318,13 +311,13 @@
 
     def finish_first(b, h, j):
         wait_bytes(midr.at[b, h, j], mr.at[b, h, j])
-        sl, fi = spot(h, j, 0)
+        xx, zz = spot(h, j, 0)
         total = pair_sum(b, h, j, 0)
-        own[b, h, sl, fi] = total + midr[b, h, j, 0].astype(F32) + midr[b, h, j, 1].astype(F32)
+        own[b, xx, h, zz] = total + midr[b, h, j, 0].astype(F32) + midr[b, h, j, 1].astype(F32)
 
     def first_sum(b, h, j):
-        sl, fi = spot(h, j, 0)
-        return own[b, h, sl, fi]
+        xx, zz = spot(h, j, 0)
+        return own[b, xx, h, zz]
 
     def send_far2(b, h):
         far2[b, h] = first_sum(b, h, 2).astype(BF16)
@@ -403,8 +396,8 @@
     first_far(0, 0)
     second_far(0, 0, 0)
     second_far(0, 1, 0)
+    first_send(1, 1)
     first_send(1, 0)
-    first_send(1, 1)
     second_send(1, 0, 0)
     second_send(1, 1, 0)
     second_far(0, 0, 1)
@@ -414,8 +407,8 @@
     gate_up(0, 0)
     second_far(0, 1, 1)
     gate_up(0, 1)
+    second_far(0, 1, 3)
     second_recv(0, 0, 2)
-    second_far(0, 1, 3)
     from_partner(0, 1)
     gate_up(1, 0)
     first_recv(1, 0)
@@ -453,111 +446,117 @@
     d_hidden(0, 0)
     second_recv(1, 1, 2)
     second_far(1, 0, 3)
+    give(0, 1)
+    second_far(1, 1, 3)
+    keep(0, 1)
+    pair_here(0, 2)
+    send_far(0, 1, 3)
+    send_far(0, 1, 1)
+    second_far(1, 0, 2)
+    send_far(0, 0, 2)
+    send_far(0, 1, 2)
+    send_far(0, 1, 0)
+    give(0, 0)
+    pair_here(0, 3)
+    send_far(0, 0, 3)
+    second_far(1, 1, 2)
+    keep(0, 0)
     d_hidden(0, 1)
-    second_far(1, 1, 3)
-    send_far(0, 0, 2)
-    give(0, 1)
-    second_far(1, 0, 2)
-    keep(0, 1)
-    send_far(0, 0, 3)
-    give(0, 0)
-    keep(0, 0)
     from_partner(1, 1)
     from_partner(1, 3)
-    second_far(1, 1, 2)
-    give_rest(0)
     d_hidden(1, 0)
     d_hidden(1, 1)
+    d_hidden(3, 0)
+    send_mid(0, 0, 2)
+    pair_here(0, 1)
+    send_mid(0, 1, 3)
     send_far(0, 0, 1)
-    send_mid(0, 0, 2)
-    d_hidden(3, 0)
+    send_mid(0, 1, 2)
+    send_mid(0, 0, 3)
+    pair_here(0, 0)
+    send_mid(0, 1, 1)
+    send_mid(0, 1, 0)
     send_far(0, 0, 0)
-    send_mid(0, 0, 3)
     from_partner(1, 2)
     d_hidden(3, 1)
-    send_far(0, 1, 2)
-    send_far(0, 1, 3)
     d_hidden(2, 0)
-    send_far(0, 1, 1)
-    send_mid(0, 0, 1)
-    send_far(0, 1, 0)
     d_hidden(2, 1)
     activate_back(0)
     activate_back(1)
+    finish_first(0, 0, 2)
+    send_far2(0, 0)
+    finish_first(0, 1, 3)
     give_ready(1)
     give(1, 2)
-    send_mid(0, 1, 2)
-    finish_first(0, 0, 2)
-    send_far2(0, 0)
-    send_mid(0, 0, 0)
-    send_mid(0, 1, 3)
-    send_mid(0, 1, 1)
+    send_mid(0, 0, 1)
     keep(1, 2)
-    finish_first(0, 0, 3)
-    send_far(1, 0, 2)
-    send_mid(0, 1, 0)
-    give(1, 3)
-    finish_first(0, 0, 1)
-    keep(1, 3)
     finish_first(0, 1, 2)
     send_far2(0, 1)
+    finish_first(0, 0, 3)
+    give(1, 3)
+    send_mid(0, 0, 0)
+    finish_first(0, 1, 1)
+    keep(1, 3)
+    pair_here(1, 2)
+    send_far(1, 0, 2)
+    send_far(1, 1, 2)
+    send_far(1, 1, 3)
+    finish_first(0, 1, 0)
+    send_far(1, 1, 0)
+    send_far(1, 1, 1)
+    finish_first(0, 0, 1)
+    give(1, 1)
+    pair_here(1, 3)
+    send_far(1, 0, 3)
+    send_mid2(0, 1)
     send_mid2(0, 0)
-    give(1, 1)
+    keep(1, 1)
     finish_first(0, 0, 0)
-    keep(1, 1)
-    finish_first(0, 1, 3)
+    give(1, 0)
     send_mid(1, 0, 2)
-    send_far(1, 0, 3)
-    give(1, 0)
     keep(1, 0)
-    finish_first(0, 1, 1)
-    send_mid2(0, 1)
+    pair_here(1, 1)
+    send_mid(1, 1, 2)
+    send_mid(1, 1, 0)
+    send_mid(1, 1, 3)
     send_far(1, 0, 1)
-    give_rest(1)
+    send_mid(1, 1, 1)
+    send_mid(1, 0, 3)
     grads_ready()
-    finish_first(0, 1, 0)
+    send_back(0)
+    pair_here(1, 0)
     send_far(1, 0, 0)
     finish_first(1, 0, 2)
     send_far2(1, 0)
     grad_x(0)
-    send_far(1, 1, 2)
-    send_mid(1, 0, 3)
-    send_far(1, 1, 3)
-    send_far(1, 1, 1)
-    send_back(0)
-    send_far(1, 1, 0)
+    send_mid(1, 0, 1)
+    finish_first(1, 1, 2)
+    send_far2(1, 1)
     grad_s(0)
-    send_mid(1, 0, 1)
+    finish_first(1, 1, 0)
+    finish_first(1, 0, 3)
     grad_x(1)
-    send_mid(1, 1, 2)
+    back_here(0)
     send_mid(1, 0, 0)
-    send_mid(1, 1, 3)
-    finish_first(1, 0, 3)
+    finish_first(1, 1, 3)
     grad_s(1)
-    send_mid(1, 1, 1)
-    back_here(0)
     grad_x(2)
     finish_first(1, 0, 1)
-    send_mid(1, 1, 0)
+    finish_first(1, 1, 1)
+    grad_s(2)
+    send_mid2(1, 1)
     send_mid2(1, 0)
-    grad_s(2)
-    finish_first(1, 1, 2)
-    send_far2(1, 1)
+    grad_x(3)
     finish_first(1, 0, 0)
-    grad_x(3)
-    finish_first(1, 1, 3)
     grad_s(3)
     grad_x(4)
     grad_s(4)
-    finish_first(1, 1, 1)
-    send_mid2(1, 1)
     grad_x(5)
-    finish_first(1, 1, 0)
+    send_back(1)
     grad_s(5)
     grad_x(6)
     grad_s(6)
     grad_x(7)
-    send_back(1)
     grad_s(7)
     back_here(1)
 
@@ -651,9 +650,9 @@
         scratch_shapes=[
             packed, packed, gather_buf, gather_buf, weight_buf, weight_buf, weight_buf,
             acc, acc, acc, hidden_buf, hidden_buf, hidden_buf,
-            pltpu.VMEM((2, 2, SIDE, SIDE, ROWS, PART), F32),
-            pltpu.VMEM((2, SIDE, SIDE, ROWS, PART), BF16),
-            pltpu.VMEM((2, 2, SIDE, SIDE, ROWS, PART), BF16),
+            pltpu.VMEM((2, SIDE, 2, SIDE, ROWS, PART), F32),
+            pltpu.VMEM((SIDE, 2, SIDE, ROWS, PART), BF16),
+            pltpu.VMEM((2, SIDE, 2, SIDE, ROWS, PART), BF16),
             pltpu.VMEM((2, 2, SIDE, ROWS, PART), BF16),
             pltpu.VMEM((2, 2, SIDE, 2, HALF, PART), BF16),
             pltpu.VMEM((2, 2, SIDE, 2, ROWS, PART), BF16),
@@ -669,7 +668,7 @@
             pltpu.VMEM((2, units, WIDE), BF16),
             dma((3,)), dma((3, 2)), dma((2,)), dma((2,)),
             dma((2, 2)), dma((2, 2)), dma((2, 2, 4)), dma((2, 2, 4)), dma((2,)), dma((2,)), dma((2, 4)),
-            dma(()), dma((2, 2, 4)), dma((2, 2, 4)), dma((2, 2, 4)), dma((2, 2)), dma((2, 2)), dma((2,)),
+            dma(()), dma((2, 4)), dma((2, 2, 4)), dma((2, 2, 4)), dma((2, 2)), dma((2, 2)), dma((2,)),
             dma((2,)), dma((2,)),
         ],
         compiler_params=pltpu.CompilerParams(collective_id=0, has_side_effects=True, vmem_limit_bytes=VMEM_LIMIT),

time: 100 us -> 94.7 us (0.947)
  Pallas kernels: 99 us -> 93.8 us
    pallas_call x1, Pallas kernels: 88.6 us -> 83.4 us  [per_device(): pl.pallas_call(main_kernel, out_shape=(grad_shape, grad_shape, grad_shape...]
where the time goes in v5:
time: 94.7 us; the launch traced here: 94.6 us
  Pallas kernels  93.8 us (99%)
    pallas_call x1, Pallas kernels, per_device(): pl.pallas_call(main_kernel, out_shape=(grad_shape, grad_shape, grad_shape...  83.4 us
    pallas_call x1, Pallas kernels, per_device(): pl.pallas_call(finish_kernel, out_shape=(token_shape, token_shape, grad_s...  10.4 us

profile of v5, /device:TPU:0, one launch (start us, length us, event | category | flops | bytes accessed | tf_op | source)
XLA Modules:
  0.0 94.6 jit_solution(11843385185097089741)
XLA Ops:
  0.6 83.4 %expert_layer.1 = (bf16[448,4096]{1,0:T(8,128)(2,1)}, bf16[448,4096]{1,0:T(8,128)(2,1)}, bf16[448,4096]{1,0:T(8,128)(2,1)}, bf16[2,4,80,256]{3,2,1,0:T(8,128)(2,1)}) custom-call(s32[2,128]{1,0:T(2,128)} %bitcast.2, f32[2,128]{1,0:T(2,128)} %bitcast.4, bf16[128,512]{1,0:T(8,128)(2,1)} %tok.1, bf16[128,512]{1,0:T(8,128)(2,1)} %cot.1, bf16[448,4096]{1,0:T(8,128)(2,1)} %wg.1, ...), custom_call_target="tpu_custom_call" | custom-call | tf_op jit(solution)/shard_map/expert_layer/pallas_call | solution.py:645
  84.0 10.4 %finish.1 = (bf16[128,512]{1,0:T(8,128)(2,1)}, bf16[128,512]{1,0:T(8,128)(2,1)}, bf16[448,4096]{1,0:T(8,128)(2,1)}, bf16[448,4096]{1,0:T(8,128)(2,1)}, bf16[448,4096]{1,0:T(8,128)(2,1)}) custom-call(s32[2,128]{1,0:T(2,128)} %bitcast.3, f32[2,128]{1,0:T(2,128)} %bitcast.5, bf16[2,4,80,256]{3,2,1,0:T(8,128)(2,1)} %get-tuple-element.9.back, ...), custom_call_target="tpu_custom_call" | custom-call | tf_op jit(solution)/shard_map/finish/pallas_call | solution.py:679

commit v6 on v5

--- a/solution.py
+++ b/solution.py
@@ -380,184 +380,184 @@
     assemble(0)
     first_send(0, 1)
     first_send(0, 0)
+    second_send(0, 1, 0)
     second_send(0, 0, 0)
-    second_send(0, 1, 0)
+    first_recv(0, 1)
     gate_ready()
-    assemble(1)
-    first_recv(0, 1)
     first_recv(0, 0)
     second_recv(0, 0, 0)
-    second_recv(0, 1, 0)
     first_far(0, 1)
     second_recv(0, 1, 1)
+    assemble(1)
+    second_recv(0, 1, 0)
     second_recv(0, 0, 1)
+    first_far(0, 0)
+    second_recv(0, 0, 3)
+    second_far(0, 0, 0)
     second_recv(0, 1, 3)
-    second_recv(0, 0, 3)
-    first_far(0, 0)
-    second_far(0, 0, 0)
-    second_far(0, 1, 0)
     first_send(1, 1)
-    first_send(1, 0)
-    second_send(1, 0, 0)
-    second_send(1, 1, 0)
     second_far(0, 0, 1)
     second_recv(0, 1, 2)
-    second_far(0, 0, 3)
+    first_send(1, 0)
+    second_send(1, 1, 0)
     from_partner(0, 0)
     gate_up(0, 0)
+    second_recv(0, 0, 2)
+    second_send(1, 0, 0)
+    gate_up(0, 1)
+    second_far(0, 1, 0)
+    second_far(0, 1, 3)
+    second_far(0, 0, 3)
+    from_partner(0, 1)
     second_far(0, 1, 1)
-    gate_up(0, 1)
-    second_far(0, 1, 3)
-    second_recv(0, 0, 2)
-    from_partner(0, 1)
     gate_up(1, 0)
+    second_far(0, 1, 2)
+    first_recv(1, 1)
     first_recv(1, 0)
-    first_recv(1, 1)
+    second_far(0, 0, 2)
+    gate_up(1, 1)
     from_partner(0, 3)
-    gate_up(1, 1)
+    gate_up(3, 0)
+    second_recv(1, 0, 0)
+    gate_up(3, 1)
+    first_far(1, 1)
     second_recv(1, 1, 0)
-    second_recv(1, 0, 0)
-    gate_up(3, 0)
-    second_far(0, 0, 2)
-    second_far(0, 1, 2)
-    gate_up(3, 1)
-    first_far(1, 0)
-    second_recv(1, 0, 1)
-    second_recv(1, 1, 1)
     from_partner(0, 2)
     gate_up(2, 0)
+    gate_up(2, 1)
+    second_recv(1, 1, 1)
+    second_recv(1, 0, 1)
+    second_recv(1, 1, 3)
+    activate(0)
     second_recv(1, 0, 3)
-    gate_up(2, 1)
-    first_far(1, 1)
-    second_recv(1, 1, 3)
-    second_far(1, 1, 0)
-    activate(0)
+    first_far(1, 0)
+    activate(1)
+    give_ready(0)
     second_far(1, 0, 0)
-    activate(1)
-    second_far(1, 1, 1)
-    give_ready(0)
     give(0, 2)
     keep(0, 2)
+    give(0, 3)
+    second_recv(1, 1, 2)
+    second_far(1, 0, 1)
+    keep(0, 3)
+    give(0, 1)
+    keep(0, 1)
+    second_far(1, 0, 3)
+    from_partner(1, 0)
+    second_far(1, 1, 1)
+    second_far(1, 1, 0)
+    d_hidden(0, 0)
+    give(0, 0)
+    pair_here(0, 2)
     second_recv(1, 0, 2)
-    give(0, 3)
-    keep(0, 3)
-    second_far(1, 0, 1)
-    from_partner(1, 0)
-    d_hidden(0, 0)
-    second_recv(1, 1, 2)
-    second_far(1, 0, 3)
-    give(0, 1)
-    second_far(1, 1, 3)
-    keep(0, 1)
-    pair_here(0, 2)
-    send_far(0, 1, 3)
-    send_far(0, 1, 1)
-    second_far(1, 0, 2)
     send_far(0, 0, 2)
     send_far(0, 1, 2)
+    second_far(1, 1, 3)
+    send_far(0, 1, 1)
+    d_hidden(0, 1)
+    send_far(0, 1, 3)
     send_far(0, 1, 0)
-    give(0, 0)
     pair_here(0, 3)
+    second_far(1, 1, 2)
     send_far(0, 0, 3)
-    second_far(1, 1, 2)
-    keep(0, 0)
-    d_hidden(0, 1)
     from_partner(1, 1)
-    from_partner(1, 3)
     d_hidden(1, 0)
     d_hidden(1, 1)
+    pair_here(0, 1)
+    keep(0, 0)
+    second_far(1, 0, 2)
+    send_far(0, 0, 1)
+    from_partner(1, 3)
     d_hidden(3, 0)
+    d_hidden(3, 1)
     send_mid(0, 0, 2)
-    pair_here(0, 1)
+    send_mid(0, 1, 2)
+    pair_here(0, 0)
+    send_far(0, 0, 0)
+    send_mid(0, 0, 3)
     send_mid(0, 1, 3)
-    send_far(0, 0, 1)
-    send_mid(0, 1, 2)
-    send_mid(0, 0, 3)
-    pair_here(0, 0)
-    send_mid(0, 1, 1)
-    send_mid(0, 1, 0)
-    send_far(0, 0, 0)
     from_partner(1, 2)
-    d_hidden(3, 1)
     d_hidden(2, 0)
     d_hidden(2, 1)
     activate_back(0)
     activate_back(1)
-    finish_first(0, 0, 2)
-    send_far2(0, 0)
-    finish_first(0, 1, 3)
     give_ready(1)
     give(1, 2)
+    send_mid(0, 1, 0)
+    keep(1, 2)
+    give(1, 3)
     send_mid(0, 0, 1)
-    keep(1, 2)
+    keep(1, 3)
+    give(1, 1)
+    pair_here(1, 2)
+    send_far(1, 1, 2)
+    send_far(1, 0, 2)
+    send_mid(0, 1, 1)
+    send_mid(0, 0, 0)
+    keep(1, 1)
+    pair_here(1, 3)
+    give(1, 0)
+    send_far(1, 0, 3)
+    send_far(1, 1, 3)
+    keep(1, 0)
+    send_mid(1, 0, 2)
+    finish_first(0, 0, 2)
+    send_far(1, 1, 1)
+    pair_here(1, 1)
+    send_far(1, 0, 1)
+    send_mid(1, 1, 2)
+    grads_ready()
+    finish_first(0, 1, 3)
+    pair_here(1, 0)
+    finish_first(0, 1, 1)
+    send_far2(0, 0)
+    send_mid(1, 0, 3)
+    send_mid(1, 1, 3)
+    finish_first(0, 0, 0)
+    send_far(1, 1, 0)
     finish_first(0, 1, 2)
+    send_far(1, 0, 0)
+    send_mid(1, 1, 1)
     send_far2(0, 1)
+    finish_first(0, 1, 0)
+    grad_x(0)
     finish_first(0, 0, 3)
-    give(1, 3)
-    send_mid(0, 0, 0)
-    finish_first(0, 1, 1)
-    keep(1, 3)
-    pair_here(1, 2)
-    send_far(1, 0, 2)
-    send_far(1, 1, 2)
-    send_far(1, 1, 3)
-    finish_first(0, 1, 0)
-    send_far(1, 1, 0)
-    send_far(1, 1, 1)
-    finish_first(0, 0, 1)
-    give(1, 1)
-    pair_here(1, 3)
-    send_far(1, 0, 3)
-    send_mid2(0, 1)
-    send_mid2(0, 0)
-    keep(1, 1)
-    finish_first(0, 0, 0)
-    give(1, 0)
-    send_mid(1, 0, 2)
-    keep(1, 0)
-    pair_here(1, 1)
-    send_mid(1, 1, 2)
-    send_mid(1, 1, 0)
-    send_mid(1, 1, 3)
-    send_far(1, 0, 1)
-    send_mid(1, 1, 1)
-    send_mid(1, 0, 3)
-    grads_ready()
-    send_back(0)
-    pair_here(1, 0)
-    send_far(1, 0, 0)
+    grad_s(0)
+    finish_first(1, 1, 2)
+    send_mid(1, 0, 1)
     finish_first(1, 0, 2)
     send_far2(1, 0)
-    grad_x(0)
-    send_mid(1, 0, 1)
-    finish_first(1, 1, 2)
     send_far2(1, 1)
-    grad_s(0)
-    finish_first(1, 1, 0)
+    finish_first(0, 0, 1)
+    grad_x(1)
     finish_first(1, 0, 3)
-    grad_x(1)
-    back_here(0)
+    grad_s(1)
+    send_mid2(0, 0)
+    send_mid2(0, 1)
+    send_mid(1, 1, 0)
+    grad_x(2)
+    finish_first(1, 0, 1)
     send_mid(1, 0, 0)
     finish_first(1, 1, 3)
-    grad_s(1)
-    grad_x(2)
-    finish_first(1, 0, 1)
     finish_first(1, 1, 1)
     grad_s(2)
+    send_mid2(1, 0)
     send_mid2(1, 1)
-    send_mid2(1, 0)
     grad_x(3)
-    finish_first(1, 0, 0)
+    send_back(0)
     grad_s(3)
     grad_x(4)
     grad_s(4)
+    finish_first(1, 0, 0)
     grad_x(5)
+    finish_first(1, 1, 0)
     send_back(1)
     grad_s(5)
     grad_x(6)
     grad_s(6)
     grad_x(7)
     grad_s(7)
+    back_here(0)
     back_here(1)
 
     for k in (ETS - 2, ETS - 1):

time: 94.7 us -> 91.1 us (0.962)
  Pallas kernels: 93.8 us -> 90.1 us
    pallas_call x1, Pallas kernels: 83.4 us -> 79.8 us  [per_device(): pl.pallas_call(main_kernel, out_shape=(grad_shape, grad_shape, grad_shape...]
where the time goes in v6:
time: 91.1 us; the launch traced here: 90.9 us
  Pallas kernels  90.1 us (99%)
    pallas_call x1, Pallas kernels, per_device(): pl.pallas_call(main_kernel, out_shape=(grad_shape, grad_shape, grad_shape...  79.8 us
    pallas_call x1, Pallas kernels, per_device(): pl.pallas_call(finish_kernel, out_shape=(token_shape, token_shape, grad_s...  10.4 us

profile of v6, /device:TPU:0, one launch (start us, length us, event | category | flops | bytes accessed | tf_op | source)
XLA Modules:
  0.0 90.9 jit_solution(13081451916005968135)
XLA Ops:
  0.6 79.8 %expert_layer.1 = (bf16[448,4096]{1,0:T(8,128)(2,1)}, bf16[448,4096]{1,0:T(8,128)(2,1)}, bf16[448,4096]{1,0:T(8,128)(2,1)}, bf16[2,4,80,256]{3,2,1,0:T(8,128)(2,1)}) custom-call(s32[2,128]{1,0:T(2,128)} %bitcast.2, f32[2,128]{1,0:T(2,128)} %bitcast.4, bf16[128,512]{1,0:T(8,128)(2,1)} %tok.1, bf16[128,512]{1,0:T(8,128)(2,1)} %cot.1, bf16[448,4096]{1,0:T(8,128)(2,1)} %wg.1, ...), custom_call_target="tpu_custom_call" | custom-call | tf_op jit(solution)/shard_map/expert_layer/pallas_call | solution.py:645
  80.4 10.4 %finish.1 = (bf16[128,512]{1,0:T(8,128)(2,1)}, bf16[128,512]{1,0:T(8,128)(2,1)}, bf16[448,4096]{1,0:T(8,128)(2,1)}, bf16[448,4096]{1,0:T(8,128)(2,1)}, bf16[448,4096]{1,0:T(8,128)(2,1)}) custom-call(s32[2,128]{1,0:T(2,128)} %bitcast.3, f32[2,128]{1,0:T(2,128)} %bitcast.5, bf16[2,4,80,256]{3,2,1,0:T(8,128)(2,1)} %get-tuple-element.9.back, ...), custom_call_target="tpu_custom_call" | custom-call | tf_op jit(solution)/shard_map/finish/pallas_call | solution.py:679
